TPU v7x, 256 devices: a whole 4x4x8 slice. The times are simulated.
256 devices in a mesh: pool: 32 (over y, z_lo, core), tp: 8 (over x, z_hi).
Axes of the slice: x: 4, y: 4, z: 8 (z_hi: 2, z_lo: 4; z = z_hi * 4 + z_lo), core: 2. Of those that a mesh axis runs over, the one named last changes fastest.
Arguments:
- queries: bfloat16 [8192, 4096], P('pool', 'tp'), may hold values from -8 to 8
- new_key_values: bfloat16 [8192, 2048], P('pool', 'tp'), may hold values from -6 to 6
- key_value_store: bfloat16 [768, 256, 2048], P('pool', None, 'tp'), may hold values from -6 to 6
- o_weight: bfloat16 [4096, 8192], P('tp'), may hold values from -0.09375 to 0.09375
- residual: bfloat16 [8192, 8192], P(('pool', 'tp')), may hold values from -6 to 6
- hit_dev: int32 [64, 16], replicated, may hold values from 0 to 31, as said below
- hit_blk: int32 [64, 16], replicated, may hold values from 0 to 23
- prefix_len: int32 [64], replicated, may hold values from 3072 to 4096, as said below
Outputs:
- layer_out: bfloat16 [8192, 8192], P(('pool', 'tp'))
Inputs may be any that keep to these rules, and one draw needn't show every extreme that they name: `hit_dev`: within one request the 16 pool indices are distinct. So one pool index sends at most one used block to each request, and at most 2 to the 2 requests held by any one pool index. `prefix_len`: some request has the full 16 * 256 tokens.
All inputs are finite; a program needn't handle non-finite values.
Results may differ from a plain program's by a relative error of at most 0.0085.
Values may be sent and summed in bfloat16 or wider, within the bound.
A program may use at most 128 MiB of HBM per device.

v0:
```python
import jax
import jax.numpy as jnp
from jax import lax
from jax.sharding import PartitionSpec as P

HEAD_SIZE = 128
NEW_TOKEN_COUNT = 128
PREFIX_BLOCK_LEN = 256
MAXB = 16


def shards(
    queries, new_key_values, key_value_store, o_weight, residual, hit_dev, hit_blk, prefix_len
):
    npool = lax.axis_size("pool")
    me = lax.axis_index("pool")
    rdev = queries.shape[0] // NEW_TOKEN_COUNT
    kv_local = key_value_store.shape[2] // (2 * HEAD_SIZE)
    q_local = queries.shape[1] // HEAD_SIZE
    query_group = q_local // kv_local
    token_span = MAXB * PREFIX_BLOCK_LEN
    dev_rows = hit_dev.reshape(npool, rdev, MAXB)
    blk_rows = hit_blk.reshape(npool, rdev, MAXB)
    starts = jnp.arange(MAXB, dtype=jnp.int32) * PREFIX_BLOCK_LEN
    used = starts[None, None, :] < prefix_len.reshape(npool, rdev)[:, :, None]
    match = used & (dev_rows == me)
    present = jnp.any(match, axis=2)
    chosen = jnp.sum(jnp.where(match, blk_rows, 0), axis=2)
    outgoing = jnp.take(key_value_store, chosen, axis=0)
    outgoing = jnp.where(present[:, :, None, None], outgoing, jnp.zeros_like(outgoing))
    outgoing = outgoing.reshape(npool, rdev, PREFIX_BLOCK_LEN, kv_local, 2, HEAD_SIZE)
    own_keys = outgoing[:, :, :, :, 0, :].reshape(
        npool, rdev, PREFIX_BLOCK_LEN, kv_local * HEAD_SIZE
    )
    own_values = outgoing[:, :, :, :, 1, :].reshape(
        npool, rdev, PREFIX_BLOCK_LEN, kv_local * HEAD_SIZE
    )
    base = me * rdev
    lengths = lax.dynamic_slice_in_dim(prefix_len, base, rdev, 0)
    sources = lax.dynamic_slice_in_dim(hit_dev, base, rdev, 0)
    fresh_tokens = new_key_values.reshape(rdev, NEW_TOKEN_COUNT, kv_local, 2, HEAD_SIZE)
    causal = (
        jnp.arange(NEW_TOKEN_COUNT, dtype=jnp.int32)[None, :]
        <= jnp.arange(NEW_TOKEN_COUNT, dtype=jnp.int32)[:, None]
    )

    def arrange(arrived, slot):
        ordered = jnp.take(arrived[:, slot], sources[slot], axis=0)
        return ordered.reshape(token_span, kv_local, HEAD_SIZE)

    outputs = []
    keys_in, values_in = (
        lax.all_to_all(own_keys, "pool", split_axis=0, concat_axis=0, tiled=True),
        lax.all_to_all(own_values, "pool", split_axis=0, concat_axis=0, tiled=True),
    )
    for slot in range(rdev):
        keys = arrange(keys_in, slot)
        all_keys = jnp.concatenate([keys, fresh_tokens[slot, :, :, 0]], 0)
        query_rows = queries[slot * NEW_TOKEN_COUNT : (slot + 1) * NEW_TOKEN_COUNT].reshape(
            NEW_TOKEN_COUNT, kv_local, query_group, HEAD_SIZE
        )
        scores = jnp.einsum(
            "ihgd,jhd->hgij", query_rows, all_keys, preferred_element_type=jnp.float32
        ) * HEAD_SIZE ** (-0.5)
        valid = jnp.arange(token_span, dtype=jnp.int32) < lengths[slot]
        allowed = jnp.concatenate(
            [jnp.broadcast_to(valid[None, :], (NEW_TOKEN_COUNT, token_span)), causal], 1
        )
        scores = jnp.where(allowed, scores, -jnp.inf)
        rowmax = jnp.max(scores, axis=-1, keepdims=True)
        expo = jnp.exp(scores - rowmax)
        probs = expo.astype(jnp.bfloat16)
        denom = jnp.sum(expo, axis=-1)
        values = arrange(values_in, slot)
        all_values = jnp.concatenate([values, fresh_tokens[slot, :, :, 1]], 0)
        mixed = jnp.einsum("hgij,jhd->ihgd", probs, all_values, preferred_element_type=jnp.float32)
        mixed = mixed / jnp.transpose(denom, (2, 0, 1))[..., None]
        outputs.append(mixed.reshape(NEW_TOKEN_COUNT, q_local * HEAD_SIZE).astype(jnp.bfloat16))
    attn = jnp.concatenate(outputs, 0)
    mine = lax.psum_scatter(
        jnp.dot(attn, o_weight, preferred_element_type=jnp.float32).astype(jnp.bfloat16),
        "tp",
        scatter_dimension=0,
        tiled=True,
    ).astype(jnp.float32)
    return (mine + residual.astype(jnp.float32)).astype(jnp.bfloat16)


def solution(mesh):
    placed = (
        P("pool", "tp"),
        P("pool", "tp"),
        P("pool", None, "tp"),
        P("tp", None),
        P(("pool", "tp"), None),
        P(),
        P(),
        P(),
    )
    return jax.shard_map(
        shards, mesh=mesh, in_specs=placed, out_specs=P(("pool", "tp"), None), check_vma=False
    )
```

profile of v0, /device:TPU:4, one launch (start us, length us, event | category | flops | bytes accessed | tf_op | source)
XLA Modules:
  0.0 418.1 jit_solution(12713539222415636368)
XLA Ops:
  6.5 0.0 copy-start
  6.5 0.9 fusion.46
  7.5 0.7 select_reduce_fusion
  8.2 0.1 reduce_sum.37
  8.3 0.1 reduce_sum.36
  8.5 0.1 reshape.196
  8.6 0.0 copy-done
  8.6 5.4 %gather_fusion = bf16[64,256,256]{2,1,0:T(8,128)(2,1)} fusion(bf16[24,256,256]{2,1,0:T(8,128)(2,1)S(1)} %copy-done, s32[1024]{0:T(1024)S(1)} %pad_clamp_fusion.2), kind=kCustom, calls=%fused_computation.4 | custom fusion | bytes 16777472 | tf_op jit(solution)/shard_map/jit(_take)/gather | solution.py:29
  14.0 11.9 %copy.57 = bf16[64,256,256]{1,2,0:T(8,128)(2,1)} copy(bf16[64,256,256]{2,1,0:T(8,128)(2,1)} %gather_fusion) | data formatting | bytes 16777216 | tf_op jit(solution)/shard_map/jit(_take)/gather | solution.py:29
  25.9 0.1 broadcast_in_dim.68
  26.0 7.6 %select_select_fusion = bf16[32,2,256,1,2,128]{2,5,4,1,0,3:T(8,128)(2,1)} fusion(bf16[32,2,256,1,2,128]{2,5,4,1,0,3:T(8,128)(2,1)} %bitcast.108, pred[32,2]{1,0:T(8,128)(4,1)S(1)} %compare_and_fusion, pred[32,2]{1,0:T(8,128)(4,1)S(1)} %broadcast_in_dim.68), kind=kLoop, calls=%fused_computation.10 | loop fusion | flops 8388608 | bytes 16777344 | tf_op jit(solution)/shard_map/jit(_where)/select_n | solution.py:30
  33.6 5.9 %fusion.47 = (bf16[32,2,256,1,1,128]{2,5,4,1,0,3:T(8,128)(2,1)}, bf16[32,2,256,1,1,128]{2,5,4,1,0,3:T(8,128)(2,1)}) fusion(bf16[32,2,256,1,2,128]{2,5,4,1,0,3:T(8,128)(2,1)} %select_select_fusion), kind=kLoop, calls=%fused_computation.79 | loop fusion | bytes 16777216 | tf_op jit(solution)/shard_map/slice | solution.py:35
  39.5 6.4 %copy.58 = bf16[32,2,256,1,1,128]{5,2,1,0,4,3:T(8,128)(2,1)} copy(bf16[32,2,256,1,1,128]{2,5,4,1,0,3:T(8,128)(2,1)} %get-tuple-element.10) | data formatting | bytes 8388608 | tf_op jit(solution)/shard_map/slice | solution.py:35
  46.0 9.1 %all-to-all-start = ((bf16[32,2,256,128]{3,2,1,0:T(8,128)(2,1)}), bf16[32,2,256,128]{3,2,1,0:T(8,128)(2,1)}, u32[]{:S(2)}, u32[]{:S(2)}) async-start(bf16[32,2,256,128]{3,2,1,0:T(8,128)(2,1)} %bitcast.110), calls=%async_computation | async-start | bytes 8388608 | tf_op jit(solution)/shard_map/all_to_all | solution.py:54
  55.1 6.5 %copy.62 = bf16[32,2,256,1,1,128]{5,2,1,0,4,3:T(8,128)(2,1)} copy(bf16[32,2,256,1,1,128]{2,5,4,1,0,3:T(8,128)(2,1)} %get-tuple-element.11) | data formatting | bytes 8388608 | tf_op jit(solution)/shard_map/slice | solution.py:32
  61.5 88.9 %all-to-all-done = bf16[32,2,256,128]{3,2,1,0:T(8,128)(2,1)} async-done(((bf16[32,2,256,128]{3,2,1,0:T(8,128)(2,1)}), bf16[32,2,256,128]{3,2,1,0:T(8,128)(2,1)}, u32[]{:S(2)}, u32[]{:S(2)}) %all-to-all-start) | async-done | bytes 4194336 | tf_op jit(solution)/shard_map/all_to_all | solution.py:54
  150.5 5.0 %all-to-all-start.1 = ((bf16[32,2,256,128]{3,2,1,0:T(8,128)(2,1)}), bf16[32,2,256,128]{3,2,1,0:T(8,128)(2,1)}, u32[]{:S(2)}, u32[]{:S(2)}) async-start(bf16[32,2,256,128]{3,2,1,0:T(8,128)(2,1)} %bitcast.109), calls=%async_computation.1 | async-start | bytes 8388608 | tf_op jit(solution)/shard_map/all_to_all | solution.py:53
  155.5 0.0 reduce-scatter.2.cloned.1.call-start
  155.5 0.0 copy-done.8
  155.5 0.1 dynamic_slice.7
  155.6 0.6 fusion.50
  156.2 0.7 iota_compare_fusion.2
  156.9 0.6 iota_compare_fusion.1
  157.5 0.0 copy-done.6
  157.6 0.0 copy-done.5
  157.6 0.1 copy.83
  157.8 0.2 fusion.49
  158.0 0.1 copy.81
  158.1 0.1 copy.87
  158.2 0.1 copy.85
  158.3 0.0 copy-done.7
  158.3 0.2 dynamic-slice_reduce_fusion.1
  158.6 5.0 %pad_add_fusion.1 = (pred[128,4224]{0,1:T(8,128)(4,1)}, pred[128,4224]{0,1:T(8,128)(4,1)}) fusion(pred[128,128]{0,1:T(8,128)(4,1)S(1)} %iota_compare_fusion, pred[4224]{0:T(1024)(128)(4,1)S(1)} %pad.10.clone, pred[4224]{0:T(1024)(128)(4,1)S(1)} %pad.4.clone), kind=kLoop, calls=%fused_computation.22 | loop fusion | flops 1081344 | bytes 1106176 | tf_op jit(solution)/shard_map/concatenate | solution.py:66
  163.6 4.1 slice_bitcast_fusion.3
  167.7 2.3 gather_fusion.1
  170.0 80.8 %all-to-all-done.1 = bf16[32,2,256,128]{3,2,1,0:T(8,128)(2,1)} async-done(((bf16[32,2,256,128]{3,2,1,0:T(8,128)(2,1)}), bf16[32,2,256,128]{3,2,1,0:T(8,128)(2,1)}, u32[]{:S(2)}, u32[]{:S(2)}) %all-to-all-start.1) | async-done | bytes 4194336 | tf_op jit(solution)/shard_map/all_to_all | solution.py:53
  250.9 4.7 %slice_bitcast_fusion.2 = (bf16[32,256,128]{2,1,0:T(8,128)(2,1)}, bf16[32,256,128]{2,1,0:T(8,128)(2,1)}) fusion(bf16[32,2,256,128]{3,2,1,0:T(8,128)(2,1)} %all-to-all-done.1), kind=kLoop, calls=%fused_computation.25 | loop fusion | bytes 8388608 | tf_op jit(solution)/shard_map/squeeze | solution.py:48
  255.6 3.2 gather_fusion.2
  258.8 2.8 broadcast_select_fusion.3
  261.7 2.3 copy.78
  263.9 0.7 gather_fusion.3
  264.7 2.3 gather_fusion.4
  267.0 1.6 broadcast_select_fusion.1
  268.6 1.7 copy.79
  270.3 2.6 fusion.52
  272.9 0.0 copy-start.3
  272.9 0.0 copy-start.4
  272.9 1.1 fusion
  274.1 0.1 copy-done.3
  274.1 0.1 copy-done.4
  274.3 1.3 fusion.51
  275.6 0.0 copy-start.2
  275.6 1.1 fusion.2
  276.7 0.1 copy-done.2
  276.8 1.6 fusion.27
  278.5 0.0 slice-start.1
  278.5 1.6 fusion.21
  280.1 0.0 slice-done
  280.1 0.7 slice-done.1
  280.8 4.5 %convolution_convert_fusion = bf16[256,8192]{1,0:T(8,128)(2,1)} fusion(bf16[512,8192]{1,0:T(8,128)(2,1)S(1)} %bitcast.112, bf16[128,512]{0,1:T(8,128)(2,1)S(1)} %bitcast.118, bf16[128,512]{0,1:T(8,128)(2,1)S(1)} %bitcast.117), kind=kOutput, calls=%fused_computation.5 | convolution fusion | flops 2150105088 | bytes 12845056 | tf_op jit(solution)/shard_map/dot_general | solution.py:81
  285.2 0.0 reduce-scatter.2.cloned.1.call-update
  285.3 123.9 %reduce-scatter.2.cloned.1.call-done = bf16[32,8192]{1,0:T(8,128)(2,1)} async-done(((bf16[256,8192]{1,0:T(8,128)(2,1)}), bf16[32,8192]{1,0:T(8,128)(2,1)}) %reduce-scatter.2.cloned.1.call-update) | async-done | bytes 524304 | tf_op jit(solution)/shard_map/reduce_scatter | solution.py:80
  409.1 2.1 add_convert_fusion
  411.3 0.0 copy-done.1
  (21 shorter events, 0.2 us)
Async XLA Ops:
  6.5 2.0 copy-start
  46.0 104.5 %all-to-all-start = ((bf16[32,2,256,128]{3,2,1,0:T(8,128)(2,1)}), bf16[32,2,256,128]{3,2,1,0:T(8,128)(2,1)}, u32[]{:S(2)}, u32[]{:S(2)}) async-start(bf16[32,2,256,128]{3,2,1,0:T(8,128)(2,1)} %bitcast.110), calls=%async_computation | async-start | bytes 8388608 | tf_op jit(solution)/shard_map/all_to_all | solution.py:54
  150.4 5.1 %copy-start.8 = (s32[64]{0:T(128)S(1)}, s32[64]{0:T(128)}, u32[]{:S(2)}) copy-start(s32[64]{0:T(128)} %param.17) | copy-start | bytes 772
  150.5 7.1 %copy-start.6 = (bf16[256,256]{1,0:T(8,128)(2,1)S(1)}, bf16[256,256]{1,0:T(8,128)(2,1)}, u32[]{:S(2)}) copy-start(bf16[256,256]{1,0:T(8,128)(2,1)} %param.11) | copy-start | bytes 393220
  150.5 7.1 %copy-start.5 = (bf16[256,512]{1,0:T(8,128)(2,1)S(1)}, bf16[256,512]{1,0:T(8,128)(2,1)}, u32[]{:S(2)}) copy-start(bf16[256,512]{1,0:T(8,128)(2,1)} %param.10) | copy-start | bytes 786436
  150.5 7.9 %copy-start.7 = (s32[64,16]{0,1:T(8,128)S(1)}, s32[64,16]{0,1:T(8,128)}, u32[]{:S(2)}) copy-start(s32[64,16]{0,1:T(8,128)} %param.15) | copy-start | bytes 12292
  150.5 100.4 %all-to-all-start.1 = ((bf16[32,2,256,128]{3,2,1,0:T(8,128)(2,1)}), bf16[32,2,256,128]{3,2,1,0:T(8,128)(2,1)}, u32[]{:S(2)}, u32[]{:S(2)}) async-start(bf16[32,2,256,128]{3,2,1,0:T(8,128)(2,1)} %bitcast.109), calls=%async_computation.1 | async-start | bytes 8388608 | tf_op jit(solution)/shard_map/all_to_all | solution.py:53
  155.5 253.7 %reduce-scatter.2.cloned.1.call-start = ((), (), s32[]{:S(2)}) async-start(), calls=%async_computation.3 | async-start | bytes 4718592 | tf_op jit(solution)/shard_map/reduce_scatter | solution.py:80
  272.9 1.2 copy-start.3
  272.9 1.4 copy-start.4
  275.6 1.2 copy-start.2
  276.8 3.3 slice-start
  278.5 2.3 slice-start.1
  280.8 130.5 %copy-start.1 = (bf16[24,256,256]{2,1,0:T(8,128)(2,1)S(1)}, bf16[24,256,256]{2,1,0:T(8,128)(2,1)}, u32[]{:S(2)}) copy-start(bf16[24,256,256]{2,1,0:T(8,128)(2,1)} %param.12) | copy-start | bytes 9437188
Sparse Core Ops, SparseCore 0:
  285.4 123.7 reduce-scatter.1
where the time goes:
time: 421 us; the launch traced here: 418 us
  waiting for transfers between devices  294 us (70%)
  local copies, waits for them, and re-layouts  60.4 us (14%)
  other arithmetic  24.5 us (6%)
  starting transfers between devices  14.1 us (3%)
  between operations  13.7 us (3%)
  matrix products  11.7 us (3%)
    reduce_scatter x1, waiting for transfers between devices, shards(): lax.psum_scatter(jnp.dot(attn, o_weight, preferred_element_type=jnp.float...  124 us
    all_to_all x1, waiting for transfers between devices, shards(): lax.all_to_all(own_values, 'pool', split_axis=0, concat_axis=0, tiled=True)  88.9 us
    all_to_all x1, waiting for transfers between devices, shards(): lax.all_to_all(own_keys, 'pool', split_axis=0, concat_axis=0, tiled=True)  80.8 us
    gather x2, local copies, waits for them, and re-layouts, shards(): outgoing = jnp.take(key_value_store, chosen, axis=0)  17.3 us
    slice x2, local copies, waits for them, and re-layouts, shards(): outgoing[:, :, :, :, 1, :]  12.4 us
    all_to_all x1, starting transfers between devices, shards(): lax.all_to_all(own_values, 'pool', split_axis=0, concat_axis=0, tiled=True)  9.07 us
    squeeze x2, local copies, waits for them, and re-layouts, arrange(): ordered = jnp.take(arrived[:, slot], sources[slot], axis=0)  8.78 us
    gather x4, local copies, waits for them, and re-layouts, arrange(): ordered = jnp.take(arrived[:, slot], sources[slot], axis=0)  8.67 us
  transfers between devices with their start and end apart: 3, of which 3 were waited for; matrix products, arithmetic and copies ran while one was open for 5% of the time, Pallas kernels for 0%

commit v1 on v0

v1 whole, which is shorter than its diff:
```python
import functools
import math

import jax
import jax.numpy as jnp
from jax import lax
from jax.experimental import pallas as pl
from jax.experimental.pallas import tpu as pltpu
from jax.sharding import PartitionSpec as P

HEAD = 128
NEW = 128
BLOCK = 256
MAXB = 16
NY = 4
NZ = 4
SLOTS = 4
LOG2_SCALE = HEAD**-0.5 * math.log2(math.e)
FLOOR = -1e30
ROWS = 144
MESH = pl.DeviceIdType.MESH


def nt(a, b):
    return lax.dot_general(a, b, (((1,), (1,)), ((), ())), preferred_element_type=jnp.float32)


def stacked(q):
    return jnp.concatenate([q[:, :HEAD], q[:, HEAD:]], axis=0)


def put(ref, at, o, m, l):
    ref[at + (slice(0, HEAD), slice(None))] = o.astype(jnp.bfloat16)
    high = l.astype(jnp.bfloat16).astype(jnp.float32)
    row = lax.broadcasted_iota(jnp.int32, (16, 2 * NEW), 0)
    stats = jnp.where(row == 0, m, jnp.where(row == 1, high, jnp.where(row == 2, l - high, 0.0)))
    ref[at + (slice(HEAD, ROWS), slice(None))] = stats.astype(jnp.bfloat16)


def get(ref, at):
    o = ref[at + (slice(0, HEAD), slice(None))].astype(jnp.float32)
    stats = ref[at + (slice(HEAD, ROWS), slice(None))].astype(jnp.float32)
    return o, stats[0:1], stats[1:2] + stats[2:3]


def merge(parts):
    m = functools.reduce(jnp.maximum, [p[1] for p in parts])
    o, l = 0.0, 0.0
    for po, pm, ps in parts:
        w = jnp.exp2(pm - m)
        o, l = o + po * w, l + ps * w
    return o, m, l


def attention_kernel(
    tab, q_ref, nkv_ref, kv_ref, out_ref,
    qbuf, k_sib, vt_own, vt_sib, nkv, part, r2, r1, rz, att, land,
    kv_send, kv_recv, nk_local,
    qz_send, qz_recv, qy_send, qy_recv, qr_send, qr_recv,
    p2_send, p2_recv, p1_send, p1_recv, pz_send, pz_recv, at_send, at_recv,
):
    me = lax.axis_index("pool")
    core = lax.rem(me, 2)
    mz = lax.rem(lax.div(me, 2), NZ)
    my = lax.div(me, 2 * NZ)
    up, down = lax.rem(my + 1, NY), lax.rem(my + NY - 1, NY)
    across = lax.rem(my + 2, NY)
    sib = 1 - core

    def dev(y, z, c):
        return (y * NZ + z) * 2 + c

    def remote(src, dst, send, recv, to):
        return pltpu.make_async_remote_copy(
            src_ref=src, dst_ref=dst, send_sem=send, recv_sem=recv, device_id={"pool": to}, device_id_type=MESH
        )

    barrier = pltpu.get_barrier_semaphore()
    partners = [dev(my, lax.rem(mz + k, NZ), c) for k in range(1, NZ) for c in range(2)]
    partners += [dev(my, mz, sib), dev(up, mz, core), dev(down, mz, core)]
    for p in partners:
        pl.semaphore_signal(barrier, inc=1, device_id={"pool": p}, device_id_type=MESH)
    pl.semaphore_wait(barrier, len(partners))

    def half(c):
        return pl.ds(pl.multiple_of(c * 2 * HEAD, 2 * HEAD), 2 * HEAD)

    def q_z(i, k, c):
        z = lax.rem(mz + k, NZ)
        s = i * 2 + core
        return remote(
            q_ref.at[pl.ds(i * NEW, NEW), half(c)], qbuf.at[s, my, mz],
            qz_send.at[i, k, c], qz_recv.at[s, mz], dev(my, z, c),
        )

    def q_sib(i):
        s = i * 2 + core
        return remote(
            q_ref.at[pl.ds(i * NEW, NEW), half(sib)], qbuf.at[s, my, mz],
            qz_send.at[i, 0, 0], qz_recv.at[s, mz], dev(my, mz, sib),
        )

    def q_own(i):
        s = i * 2 + core
        return pltpu.make_async_copy(
            q_ref.at[pl.ds(i * NEW, NEW), half(core)], qbuf.at[s, my, mz], qz_recv.at[s, mz]
        )

    nk_copy = remote(nkv_ref, nkv.at[core], kv_send.at[0], kv_recv.at[0], dev(my, mz, sib))
    k_copy = remote(kv_ref.at[:, :, pl.ds(0, HEAD)], k_sib, kv_send.at[1], kv_recv.at[1], dev(my, mz, sib))
    v_copy = remote(vt_own, vt_sib, kv_send.at[2], kv_recv.at[2], dev(my, mz, sib))
    nk_own = pltpu.make_async_copy(nkv_ref, nkv.at[core], nk_local)

    for i in range(2):
        for k in range(1, NZ):
            for c in range(2):
                q_z(i, k, c).start()
        q_sib(i).start()
        q_own(i).start()
    k_copy.start()
    nk_copy.start()
    nk_own.start()

    @pl.loop(0, kv_ref.shape[0])
    def _(b):
        vt_own[b] = kv_ref[b, :, HEAD:].T

    v_copy.start()

    def q_y(s, d):
        to = (up, down)[d]
        return remote(
            qbuf.at[s, my], qbuf.at[s, my], qy_send.at[s, d], qy_recv.at[s, d], dev(to, mz, core)
        )

    def q_relay(s, d):
        to, of = ((up, down), (down, up))[d]
        piece = qbuf.at[s, of, pl.ds(2 * d, 2)]
        return remote(piece, piece, qr_send.at[s, d], qr_recv.at[s, d], dev(to, mz, core))

    def wait_into(ref, sem):
        pltpu.make_async_copy(ref, ref, sem).wait()

    def stage_a(s):
        for z in range(NZ):
            wait_into(qbuf.at[s, my, z], qz_recv.at[s, z])
        q_y(s, 0).start()
        q_y(s, 1).start()

    def stage_r(s):
        wait_into(qbuf.at[s, down], qy_recv.at[s, 0])
        q_relay(s, 0).start()
        wait_into(qbuf.at[s, up], qy_recv.at[s, 1])
        q_relay(s, 1).start()

    key = lax.broadcasted_iota(jnp.int32, (BLOCK, 2 * NEW), 0)

    def attend(s, y, z):
        r = dev(y, z, lax.rem(s, 2)) * 2 + lax.div(s, 2)
        q = stacked(qbuf[s, y, z])
        codes = [tab[0, r], tab[1, r]]
        blocks = [c % 32 for c in codes]
        counts = [c // 32 for c in codes]
        keys = [kv_ref[blocks[0], :, :HEAD], k_sib[blocks[1]]]
        values = [vt_own[blocks[0]], vt_sib[blocks[1]]]
        t = [jnp.where(key < n, nt(k, q) * LOG2_SCALE, -jnp.inf) for k, n in zip(keys, counts)]
        m = jnp.maximum(jnp.max(t[0], axis=0, keepdims=True), jnp.max(t[1], axis=0, keepdims=True))
        m = jnp.maximum(m, FLOOR).astype(jnp.bfloat16).astype(jnp.float32)
        e = [jnp.exp2(x - m) for x in t]
        l = jnp.sum(e[0], axis=0, keepdims=True) + jnp.sum(e[1], axis=0, keepdims=True)
        o = [
            jnp.dot(v, x.astype(jnp.bfloat16), preferred_element_type=jnp.float32)
            for v, x in zip(values, e)
        ]
        put(part, (s, y, z), o[0] + o[1], m, l)

    def attend_column(s, y):
        @pl.loop(0, NZ)
        def _(z):
            attend(s, y, z)

    def p_2(s, d):
        to = (up, down)[d]
        return remote(
            part.at[s, across, pl.ds(2 * d, 2)], r2.at[s, d], p2_send.at[s, d], p2_recv.at[s, d], dev(to, mz, core)
        )

    def p_1(s, d):
        to = (up, down)[d]
        return remote(part.at[s, to], r1.at[s, d], p1_send.at[s, d], p1_recv.at[s, d], dev(to, mz, core))

    def p_z(s, k):
        z = lax.rem(mz + k, NZ)
        return remote(
            part.at[s, my, z], rz.at[s, mz], pz_send.at[s, k], pz_recv.at[s, mz], dev(my, z, core)
        )

    def stage_c(s):
        wait_into(qbuf.at[s, across, pl.ds(0, 2)], qr_recv.at[s, 0])
        wait_into(qbuf.at[s, across, pl.ds(2, 2)], qr_recv.at[s, 1])
        attend_column(s, across)
        p_2(s, 0).start()
        p_2(s, 1).start()
        attend_column(s, up)
        attend_column(s, down)

    def stage_m(s):
        for d in range(2):
            wait_into(r2.at[s, d], p2_recv.at[s, d])
            to = (up, down)[d]

            @pl.loop(0, 2)
            def _(j):
                put(part, (s, to, 2 * d + j), *merge([get(part, (s, to, 2 * d + j)), get(r2, (s, d, j))]))

            p_1(s, d).start()
        attend_column(s, my)

    def stage_h(s):
        for d in range(2):
            wait_into(r1.at[s, d], p1_recv.at[s, d])

        @pl.loop(0, NZ)
        def _(z):
            put(part, (s, my, z), *merge([get(part, (s, my, z)), get(r1, (s, 0, z)), get(r1, (s, 1, z))]))

        for k in range(1, NZ):
            p_z(s, k).start()

    def fresh(s):
        q = stacked(qbuf[s, my, mz])
        rows = nkv[lax.rem(s, 2), pl.ds(pl.multiple_of(lax.div(s, 2) * NEW, NEW), NEW), :]
        j = lax.broadcasted_iota(jnp.int32, (NEW, 2 * NEW), 0)
        i = lax.broadcasted_iota(jnp.int32, (NEW, 2 * NEW), 1) % NEW
        t = jnp.where(j <= i, nt(rows[:, :HEAD], q) * LOG2_SCALE, -jnp.inf)
        m = jnp.max(t, axis=0, keepdims=True).astype(jnp.bfloat16).astype(jnp.float32)
        e = jnp.exp2(t - m)
        o = jnp.dot(rows[:, HEAD:].T, e.astype(jnp.bfloat16), preferred_element_type=jnp.float32)
        return o, m, jnp.sum(e, axis=0, keepdims=True)

    def a_copy(s):
        i = lax.div(s, 2)
        return remote(att.at[s], land.at[i], at_send.at[i], at_recv.at[i], dev(my, mz, sib))

    def stage_f(s):
        parts = [fresh(s), get(part, (s, my, mz))]
        for k in range(1, NZ):
            z = lax.rem(mz + k, NZ)
            wait_into(rz.at[s, z], pz_recv.at[s, z])
            parts.append(get(rz, (s, z)))
        o, _, l = merge(parts)
        o = o / l
        att[s] = jnp.concatenate([o[:, :NEW].T, o[:, NEW:].T], axis=1).astype(jnp.bfloat16)

        @pl.when(lax.rem(s, 2) == core)
        def _():
            i = lax.div(s, 2)
            out_ref[pl.ds(pl.multiple_of(i * NEW, NEW), NEW), half(core)] = att[s]

        @pl.when(lax.rem(s, 2) != core)
        def _():
            a_copy(s).start()

    stage_a(0)
    stage_a(1)
    stage_r(0)
    nk_own.wait()
    for copy in (k_copy, nk_copy, v_copy):
        copy.wait_send()
    wait_into(nkv.at[sib], kv_recv.at[0])
    wait_into(k_sib, kv_recv.at[1])
    wait_into(vt_sib, kv_recv.at[2])

    @pl.loop(0, SLOTS + 2)
    def _(t):
        @pl.when(t < SLOTS)
        def _():
            stage_c(t)

        @pl.when(t + 1 < SLOTS)
        def _():
            stage_r(t + 1)

        @pl.when(t + 2 < SLOTS)
        def _():
            stage_a(t + 2)

        @pl.when(jnp.logical_and(t >= 1, t <= SLOTS))
        def _():
            stage_h(t - 1)

        @pl.when(t < SLOTS)
        def _():
            stage_m(t)

        @pl.when(t >= 2)
        def _():
            stage_f(t - 2)

    for i in range(2):
        for k in range(1, NZ):
            for c in range(2):
                q_z(i, k, c).wait_send()
        q_sib(i).wait_send()

    @pl.loop(0, SLOTS)
    def _(s):
        for d in range(2):
            q_y(s, d).wait_send()
            q_relay(s, d).wait_send()
            p_2(s, d).wait_send()
            p_1(s, d).wait_send()
        for k in range(1, NZ):
            p_z(s, k).wait_send()

    for i in range(2):
        a_copy(2 * i + sib).wait_send()
        wait_into(land.at[i], at_recv.at[i])
        out_ref[pl.ds(i * NEW, NEW), half(sib)] = land[i]


def attention(tab, queries, nkv, store):
    bf = jnp.bfloat16
    blocks = store.shape[0]
    vmem = pl.BlockSpec(memory_space=pltpu.VMEM)
    dma = pltpu.SemaphoreType.DMA
    unit = (ROWS, 2 * NEW)
    return pl.pallas_call(
        attention_kernel,
        out_shape=jax.ShapeDtypeStruct(queries.shape, bf),
        in_specs=[pl.BlockSpec(memory_space=pltpu.SMEM), vmem, vmem, vmem],
        out_specs=vmem,
        scratch_shapes=[
            pltpu.VMEM((SLOTS, NY, NZ, NEW, 2 * HEAD), bf),
            pltpu.VMEM((blocks, BLOCK, HEAD), bf),
            pltpu.VMEM((blocks, HEAD, BLOCK), bf),
            pltpu.VMEM((blocks, HEAD, BLOCK), bf),
            pltpu.VMEM((2, 2 * NEW, 2 * HEAD), bf),
            pltpu.VMEM((SLOTS, NY, NZ) + unit, bf),
            pltpu.VMEM((SLOTS, 2, 2) + unit, bf),
            pltpu.VMEM((SLOTS, 2, NZ) + unit, bf),
            pltpu.VMEM((SLOTS, NZ) + unit, bf),
            pltpu.VMEM((SLOTS, NEW, 2 * HEAD), bf),
            pltpu.VMEM((2, NEW, 2 * HEAD), bf),
            dma((3,)), dma((3,)), dma(()),
            dma((2, NZ, 2)), dma((SLOTS, NZ)),
            dma((SLOTS, 2)), dma((SLOTS, 2)), dma((SLOTS, 2)), dma((SLOTS, 2)),
            dma((SLOTS, 2)), dma((SLOTS, 2)), dma((SLOTS, 2)), dma((SLOTS, 2)),
            dma((SLOTS, NZ)), dma((SLOTS, NZ)), dma((2,)), dma((2,)),
        ],
        compiler_params=pltpu.CompilerParams(
            collective_id=0, has_side_effects=True, vmem_limit_bytes=40 * 1024 * 1024
        ),
    )(tab, queries, nkv, store)


def hit_table(hit_dev, hit_blk, prefix_len):
    me = lax.axis_index("pool")
    start = jnp.arange(MAXB, dtype=jnp.int32) * BLOCK
    count = jnp.clip(prefix_len[:, None] - start[None, :], 0, BLOCK)
    code = hit_blk + 32 * count
    return jnp.stack([jnp.sum(jnp.where(hit_dev == d, code, 0), axis=1) for d in (me, me + 1 - 2 * (me % 2))])


def shards(queries, new_key_values, key_value_store, o_weight, residual, hit_dev, hit_blk, prefix_len):
    tab = hit_table(hit_dev, hit_blk, prefix_len)
    attn = attention(tab, queries, new_key_values, key_value_store)
    mine = lax.psum_scatter(
        jnp.dot(attn, o_weight, preferred_element_type=jnp.float32).astype(jnp.bfloat16),
        "tp",
        scatter_dimension=0,
        tiled=True,
    ).astype(jnp.float32)
    return (mine + residual.astype(jnp.float32)).astype(jnp.bfloat16)


def solution(mesh):
    placed = (
        P("pool", "tp"),
        P("pool", "tp"),
        P("pool", None, "tp"),
        P("tp", None),
        P(("pool", "tp"), None),
        P(),
        P(),
        P(),
    )
    return jax.shard_map(
        shards, mesh=mesh, in_specs=placed, out_specs=P(("pool", "tp"), None), check_vma=False
    )
```

time: 421 us -> 266 us (0.63)
  waiting for transfers between devices: 294 us -> 126 us
  Pallas kernels: 0 us -> 110 us
  local copies, waits for them, and re-layouts: 60.4 us -> 3.74 us
  other arithmetic: 24.5 us -> 2.78 us
  starting transfers between devices: 14.1 us -> 0.01 us
    all_to_all x2 -> x0, waiting for transfers between devices: 170 us -> none  [the longest x1 88.9 us: shards(): lax.all_to_all(own_values, 'pool', split_axis=0, concat_axis=0, tiled=True)]
    pallas_call x0 -> x1, Pallas kernels: none -> 110 us  [attention(): pl.pallas_call(attention_kernel, out_shape=jax.ShapeDtypeStruct(queries.s...]
    gather x6 -> x0, local copies, waits for them, and re-layouts: 25.9 us -> none  [the longest x2 17.3 us: shards(): outgoing = jnp.take(key_value_store, chosen, axis=0)]
    slice x7 -> x0, local copies, waits for them, and re-layouts: 19.8 us -> none  [the longest x2 12.4 us: shards(): outgoing[:, :, :, :, 1, :]]
    all_to_all x2 -> x0, starting transfers between devices: 14.1 us -> none  [the longest x1 9.07 us: shards(): lax.all_to_all(own_values, 'pool', split_axis=0, concat_axis=0, tiled=True)]
    select_n x5 -> x0, other arithmetic: 12.1 us -> none  [the longest x1 7.63 us: shards(): jnp.where(present[:, :, None, None], outgoing, jnp.zeros_like(outgoing))]
    squeeze x3 -> x0, local copies, waits for them, and re-layouts: 8.79 us -> none  [the longest x2 8.78 us: arrange(): ordered = jnp.take(arrived[:, slot], sources[slot], axis=0)]
    dot_general x4 -> x0, matrix products: 7.22 us -> none  [the longest x2 3.93 us: shards(): jnp.einsum('ihgd,jhd->hgij', query_rows, all_keys, preferred_element_type...]
  transfers between devices with their start and end apart: 3 -> 1, of which waited for: 3 -> 1; matrix products, arithmetic and copies ran while one was open for 5% -> 0% of each run, Pallas kernels for 0% -> 0%
where the time goes in v1:
time: 266 us; the launch traced here: 264 us
  waiting for transfers between devices  126 us (47%)
  Pallas kernels  110 us (41%)
  between operations  13.4 us (5%)
  matrix products  7.72 us (3%)
  local copies, waits for them, and re-layouts  3.74 us (1%)
  other arithmetic  2.78 us (1%)
    reduce_scatter x1, waiting for transfers between devices, shards(): lax.psum_scatter(jnp.dot(attn, o_weight, preferred_element_type=jnp.float...  126 us
    pallas_call x1, Pallas kernels, attention(): pl.pallas_call(attention_kernel, out_shape=jax.ShapeDtypeStruct(queries.s...  110 us
    dot_general x1, matrix products, shards(): jnp.dot(attn, o_weight, preferred_element_type=jnp.float32)  7.72 us
  transfers between devices with their start and end apart: 1, of which 1 were waited for; matrix products, arithmetic and copies ran while one was open for 0% of the time, Pallas kernels for 0%

profile of v1, /device:TPU:4, one launch (start us, length us, event | category | flops | bytes accessed | tf_op | source)
XLA Modules:
  0.0 264.3 jit_solution(2088324162985230535)
XLA Ops:
  6.5 0.0 reduce-scatter.2.cloned.1.call-start
  6.5 0.8 select_reduce_fusion.1
  7.4 0.0 copy-start
  7.4 1.9 copy-done
  9.3 0.0 copy-start.1
  9.3 0.9 copy-done.1
  10.2 0.0 copy-start.2
  10.2 0.9 copy-done.2
  11.1 110.5 %shard_map.82 = bf16[256,512]{1,0:T(8,128)(2,1)S(1)} custom-call(s32[2,64]{1,0:T(2,128)S(1)} %pad_add_fusion.tab, bf16[256,512]{1,0:T(8,128)(2,1)S(1)} %copy-done.1, bf16[256,256]{1,0:T(8,128)(2,1)S(1)} %copy-done.2, bf16[24,256,256]{2,1,0:T(8,128)(2,1)S(1)} %copy-done), custom_call_target="tpu_custom_call" | custom-call | tf_op jit(solution)/shard_map/pallas_call | solution.py:328
  121.6 0.0 copy-start.3
  121.6 7.7 %convolution_convert_fusion = bf16[256,8192]{1,0:T(8,128)(2,1)} fusion(bf16[256,512]{1,0:T(8,128)(2,1)S(1)} %shard_map.82, bf16[512,8192]{1,0:T(8,128)(2,1)} %param.11), kind=kOutput, calls=%fused_computation | convolution fusion | flops 2149580800 | bytes 12845056 | tf_op jit(solution)/shard_map/dot_general | solution.py:369
  129.3 0.0 reduce-scatter.2.cloned.1.call-update
  129.4 126.1 %reduce-scatter.2.cloned.1.call-done = bf16[32,8192]{1,0:T(8,128)(2,1)} async-done(((bf16[256,8192]{1,0:T(8,128)(2,1)}), bf16[32,8192]{1,0:T(8,128)(2,1)}) %reduce-scatter.2.cloned.1.call-update) | async-done | bytes 524304 | tf_op jit(solution)/shard_map/reduce_scatter | solution.py:368
  255.5 0.0 copy-done.3
  255.5 2.0 add_convert_fusion
  (2 shorter events, 0.0 us)
Async XLA Ops:
  6.5 248.9 %reduce-scatter.2.cloned.1.call-start = ((), (), s32[]{:S(2)}) async-start(), calls=%async_computation.1 | async-start | bytes 4718592 | tf_op jit(solution)/shard_map/reduce_scatter | solution.py:368
  7.4 1.9 copy-start
  9.3 0.9 copy-start.1
  10.2 0.9 copy-start.2
  121.6 133.9 %copy-start.3 = (bf16[32,8192]{1,0:T(8,128)(2,1)S(1)}, bf16[32,8192]{1,0:T(8,128)(2,1)}, u32[]{:S(2)}) copy-start(bf16[32,8192]{1,0:T(8,128)(2,1)} %param.12) | copy-start | bytes 1572868
Sparse Core Ops, SparseCore 0:
  129.5 125.9 reduce-scatter.1

commit v2 on v1

v2 whole, which is shorter than its diff:
```python
import functools
import math

import jax
import jax.numpy as jnp
from jax import lax
from jax.experimental import pallas as pl
from jax.experimental.pallas import tpu as pltpu
from jax.sharding import PartitionSpec as P

HEAD = 128
NEW = 128
BLOCK = 256
MAXB = 16
NY = 4
NZ = 4
NX = 4
SLOTS = 4
CHUNKS = 2
LOG2_SCALE = HEAD**-0.5 * math.log2(math.e)
FLOOR = -1e30
ROWS = 144
MESH = pl.DeviceIdType.MESH


def nt(a, b):
    return lax.dot_general(a, b, (((1,), (1,)), ((), ())), preferred_element_type=jnp.float32)


def stacked(q):
    return jnp.concatenate([q[:, :HEAD], q[:, HEAD:]], axis=0)


def put(ref, at, o, m, l):
    ref[at + (slice(0, HEAD), slice(None))] = o.astype(jnp.bfloat16)
    high = l.astype(jnp.bfloat16).astype(jnp.float32)
    row = lax.broadcasted_iota(jnp.int32, (16, 2 * NEW), 0)
    stats = jnp.where(row == 0, m, jnp.where(row == 1, high, jnp.where(row == 2, l - high, 0.0)))
    ref[at + (slice(HEAD, ROWS), slice(None))] = stats.astype(jnp.bfloat16)


def get(ref, at):
    o = ref[at + (slice(0, HEAD), slice(None))].astype(jnp.float32)
    stats = ref[at + (slice(HEAD, ROWS), slice(None))].astype(jnp.float32)
    return o, stats[0:1], stats[1:2] + stats[2:3]


def merge(parts):
    m = functools.reduce(jnp.maximum, [p[1] for p in parts])
    o, l = 0.0, 0.0
    for po, pm, ps in parts:
        w = jnp.exp2(pm - m)
        o, l = o + po * w, l + ps * w
    return o, m, l


def layer_kernel(
    tab, q_ref, nkv_ref, kv_ref, res_ref, w_ref, out_ref,
    qbuf, k_sib, vt_own, vt_sib, nkv, part, r2, r1, rz, att,
    w, res_sib, proj, x1, x2, zout, zin, done, fin,
    kv_send, kv_recv, local,
    qz_send, qz_recv, qy_send, qy_recv, qr_send, qr_recv,
    p2_send, p2_recv, p1_send, p1_recv, pz_send, pz_recv, at_send, at_recv,
    x1_send, x1_recv, x2_send, x2_recv, zh_send, zh_recv, fin_send, fin_recv,
):
    me, tp = lax.axis_index("pool"), lax.axis_index("tp")
    core = lax.rem(me, 2)
    mz = lax.rem(lax.div(me, 2), NZ)
    my = lax.div(me, 2 * NZ)
    zh = lax.rem(tp, 2)
    mx = lax.div(tp, 2)
    up, down = lax.rem(my + 1, NY), lax.rem(my + NY - 1, NY)
    across = lax.rem(my + 2, NY)
    sib = 1 - core
    others = (mz + 1 - 2 * lax.rem(mz, 2), lax.rem(mz + 2, NZ), NZ - 1 - mz)
    pair, facing = mx + 1 - 2 * lax.rem(mx, 2), NX - 1 - mx
    width = w.shape[1]
    chunk = width // CHUNKS

    def dev(y, z, c):
        return (y * NZ + z) * 2 + c

    def tp_of(x, h):
        return x * 2 + h

    def remote(src, dst, send, recv, **to):
        return pltpu.make_async_remote_copy(
            src_ref=src, dst_ref=dst, send_sem=send, recv_sem=recv, device_id=to, device_id_type=MESH
        )

    def wait_into(ref, sem):
        pltpu.make_async_copy(ref, ref, sem).wait()

    barrier = pltpu.get_barrier_semaphore()
    partners = [{"pool": dev(my, z, c)} for z in others for c in range(2)]
    partners += [{"pool": p} for p in (dev(my, mz, sib), dev(up, mz, core), dev(down, mz, core))]
    partners += [{"tp": p} for p in (tp_of(pair, zh), tp_of(facing, zh), tp_of(mx, 1 - zh))]
    for p in partners:
        pl.semaphore_signal(barrier, inc=1, device_id=p, device_id_type=MESH)
    pl.semaphore_wait(barrier, len(partners))

    def half(c):
        return pl.ds(pl.multiple_of(c * 2 * HEAD, 2 * HEAD), 2 * HEAD)

    def columns(c):
        return pl.ds(pl.multiple_of(c * width, width), width)

    def owner(s):
        return lax.rem(s + lax.div(s, 2), 2)

    firsts = ((core, core), (sib, 2 + sib))

    def tokens(i):
        return pl.ds(pl.multiple_of(i * NEW, NEW), NEW)

    def q_z(j, k, c):
        i, s = firsts[j]
        return remote(
            q_ref.at[tokens(i), half(c)], qbuf.at[s, my, mz],
            qz_send.at[j, k, c], qz_recv.at[s, mz], pool=dev(my, others[k], c),
        )

    def q_sib(j):
        i, s = firsts[j]
        return remote(
            q_ref.at[tokens(i), half(sib)], qbuf.at[s, my, mz],
            qz_send.at[j, 3, 0], qz_recv.at[s, mz], pool=dev(my, mz, sib),
        )

    def q_own(j):
        i, s = firsts[j]
        return pltpu.make_async_copy(q_ref.at[tokens(i), half(core)], qbuf.at[s, my, mz], qz_recv.at[s, mz])

    here = dev(my, mz, sib)
    nk_copy = remote(nkv_ref, nkv.at[core], kv_send.at[0], kv_recv.at[0], pool=here)
    k_copy = remote(kv_ref.at[:, :, pl.ds(0, HEAD)], k_sib, kv_send.at[1], kv_recv.at[1], pool=here)
    v_copy = remote(vt_own, vt_sib, kv_send.at[2], kv_recv.at[2], pool=here)
    res_copy = remote(res_ref.at[:, columns(sib)], res_sib, kv_send.at[3], kv_recv.at[3], pool=here)
    nk_own = pltpu.make_async_copy(nkv_ref, nkv.at[core], local.at[0])
    w_own = pltpu.make_async_copy(w_ref.at[:, columns(core)], w, local.at[1])

    def q_y(s, d, z):
        piece = qbuf.at[s, my, z]
        return remote(piece, piece, qy_send.at[s, d, z], qy_recv.at[s, d, z], pool=dev((up, down)[d], mz, core))

    def q_relay(s, d, j):
        to, of = ((up, down), (down, up))[d]
        piece = qbuf.at[s, of, 2 * d + j]
        return remote(piece, piece, qr_send.at[s, d, j], qr_recv.at[s, d, j], pool=dev(to, mz, core))

    def z_arrived(s, z):
        wait_into(qbuf.at[s, my, z], qz_recv.at[s, z])
        q_y(s, 0, z).start()
        q_y(s, 1, z).start()

    def y_arrived(s, d, z):
        wait_into(qbuf.at[s, (down, up)[d], z], qy_recv.at[s, d, z])

    def stage_r(s):
        for j in range(2):
            for d in range(2):
                y_arrived(s, d, 2 * d + j)
                q_relay(s, d, j).start()

    for j in range(2):
        q_own(j).start()
        q_sib(j).start()
    for k in range(NZ - 1):
        for c in range(2):
            q_z(0, k, c).start()
    for s in range(2):
        z_arrived(s, mz)
    nk_own.start()
    nk_copy.start()
    k_copy.start()

    @pl.loop(0, kv_ref.shape[0])
    def _(b):
        vt_own[b] = kv_ref[b, :, HEAD:].T

    v_copy.start()
    for z in others:
        for s in range(2):
            z_arrived(s, z)
    for k in range(NZ - 1):
        for c in range(2):
            q_z(1, k, c).start()
    for s in range(2):
        z_arrived(2 + s, mz)
    res_copy.start()
    w_own.start()
    stage_r(0)

    key = lax.broadcasted_iota(jnp.int32, (BLOCK, 2 * NEW), 0)

    def attend(s, y, z):
        r = dev(y, z, owner(s)) * 2 + lax.rem(s, 2)
        q = stacked(qbuf[s, y, z])
        codes = [tab[0, r], tab[1, r]]
        blocks = [c % 32 for c in codes]
        counts = [c // 32 for c in codes]
        keys = [kv_ref[blocks[0], :, :HEAD], k_sib[blocks[1]]]
        values = [vt_own[blocks[0]], vt_sib[blocks[1]]]
        t = [jnp.where(key < n, nt(k, q) * LOG2_SCALE, -jnp.inf) for k, n in zip(keys, counts)]
        m = jnp.maximum(jnp.max(t[0], axis=0, keepdims=True), jnp.max(t[1], axis=0, keepdims=True))
        m = jnp.maximum(m, FLOOR).astype(jnp.bfloat16).astype(jnp.float32)
        e = [jnp.exp2(x - m) for x in t]
        l = jnp.sum(e[0], axis=0, keepdims=True) + jnp.sum(e[1], axis=0, keepdims=True)
        o = [
            jnp.dot(v, x.astype(jnp.bfloat16), preferred_element_type=jnp.float32)
            for v, x in zip(values, e)
        ]
        put(part, (s, y, z), o[0] + o[1], m, l)

    def p_2(s, d, j):
        return remote(
            part.at[s, across, 2 * d + j], r2.at[s, d, j],
            p2_send.at[s, d, j], p2_recv.at[s, d, j], pool=dev((up, down)[d], mz, core),
        )

    def p_1(s, d, z):
        to = (up, down)[d]
        return remote(
            part.at[s, to, z], r1.at[s, d, z], p1_send.at[s, d, z], p1_recv.at[s, d, z], pool=dev(to, mz, core)
        )

    def p_z(s, z):
        return remote(
            part.at[s, my, z], rz.at[s, mz], pz_send.at[s, z], pz_recv.at[s, mz], pool=dev(my, z, core)
        )

    def stage_c(s):
        for j in range(2):
            for d in range(2):
                wait_into(qbuf.at[s, across, 2 * d + j], qr_recv.at[s, d, j])
                y_arrived(s, d, 2 - 2 * d + j)

        @pl.loop(0, 2)
        def _(j):
            attend(s, across, j)
            attend(s, across, 2 + j)
            p_2(s, 0, j).start()
            p_2(s, 1, j).start()

        @pl.loop(0, 2)
        def _(j):
            attend(s, up, 2 + j)
            attend(s, down, j)
            p_1(s, 0, 2 + j).start()
            p_1(s, 1, j).start()

        @pl.loop(0, 2)
        def _(j):
            attend(s, up, j)
            attend(s, down, 2 + j)

    def stage_m(s):
        @pl.loop(0, 2)
        def _(j):
            for d in range(2):
                z, to = 2 * d + j, (up, down)[d]
                wait_into(r2.at[s, d, j], p2_recv.at[s, d, j])
                put(part, (s, to, z), *merge([get(part, (s, to, z)), get(r2, (s, d, j))]))
                p_1(s, d, z).start()

        @pl.loop(0, 2)
        def _(j):
            attend(s, my, j)
            attend(s, my, 2 + j)

    def stage_h(s):
        @pl.loop(0, NZ)
        def _(k):
            z = lax.rem(mz + 1 + k, NZ)
            for d in range(2):
                wait_into(r1.at[s, d, z], p1_recv.at[s, d, z])
            put(part, (s, my, z), *merge([get(part, (s, my, z)), get(r1, (s, 0, z)), get(r1, (s, 1, z))]))

            @pl.when(k < NZ - 1)
            def _():
                p_z(s, z).start()

    def fresh(s):
        q = stacked(qbuf[s, my, mz])
        rows = nkv[owner(s), tokens(lax.rem(s, 2)), :]
        j = lax.broadcasted_iota(jnp.int32, (NEW, 2 * NEW), 0)
        i = lax.broadcasted_iota(jnp.int32, (NEW, 2 * NEW), 1) % NEW
        t = jnp.where(j <= i, nt(rows[:, :HEAD], q) * LOG2_SCALE, -jnp.inf)
        m = jnp.max(t, axis=0, keepdims=True).astype(jnp.bfloat16).astype(jnp.float32)
        e = jnp.exp2(t - m)
        o = jnp.dot(rows[:, HEAD:].T, e.astype(jnp.bfloat16), preferred_element_type=jnp.float32)
        return o, m, jnp.sum(e, axis=0, keepdims=True)

    def a_copy(s):
        mine = att.at[s, :, half(core)]
        return remote(mine, mine, at_send.at[s], at_recv.at[s], pool=here)

    def stage_f(s):
        parts = [fresh(s), get(part, (s, my, mz))]
        for z in others:
            wait_into(rz.at[s, z], pz_recv.at[s, z])
            parts.append(get(rz, (s, z)))
        o, _, l = merge(parts)
        o = o / l
        att[s, :, half(core)] = jnp.concatenate([o[:, :NEW].T, o[:, NEW:].T], axis=1).astype(jnp.bfloat16)
        a_copy(s).start()

    def is_dest(s):
        return lax.div(mx, 2) == lax.rem(s, 2)

    def sent_half(s):
        return jnp.where(is_dest(s), 1 - lax.rem(mx, 2), lax.rem(mx, 2))

    def rows64(h):
        return pl.ds(pl.multiple_of(h * 64, 64), 64)

    def rows32(h, g):
        return pl.ds(pl.multiple_of(h * 64 + g * 32, 32), 32)

    def cols(n):
        return pl.ds(pl.multiple_of(n * chunk, chunk), chunk)

    def x_1(s, n):
        return remote(
            proj.at[s, rows64(sent_half(s)), cols(n)], x1.at[s, :, cols(n)],
            x1_send.at[s, n], x1_recv.at[s, n], tp=tp_of(pair, zh),
        )

    def x_2(s, n):
        return remote(
            proj.at[s, rows64(1 - sent_half(s)), cols(n)], x2.at[s, :, cols(n)],
            x2_send.at[s, n], x2_recv.at[s, n], tp=tp_of(facing, zh),
        )

    def z_h(s, n):
        return remote(
            zout.at[s, :, cols(n)], zin.at[s, :, cols(n)], zh_send.at[s, n], zh_recv.at[s, n], tp=tp_of(mx, 1 - zh)
        )

    def stage_o(s):
        @pl.when(s == 0)
        def _():
            w_own.wait()

        theirs = att.at[s, :, half(sib)]
        wait_into(theirs, at_recv.at[s])

        @pl.loop(0, CHUNKS)
        def _(n):
            proj[s, :, cols(n)] = jnp.dot(
                att[s], w[:, cols(n)], preferred_element_type=jnp.float32
            ).astype(jnp.bfloat16)
            x_1(s, n).start()

    def f32(x):
        return x.astype(jnp.float32)

    def stage_x(s):
        @pl.when(jnp.logical_not(is_dest(s)))
        def _():
            keep = 1 - sent_half(s)

            @pl.loop(0, CHUNKS)
            def _(n):
                wait_into(x1.at[s, :, cols(n)], x1_recv.at[s, n])
                total = f32(proj[s, rows64(keep), cols(n)]) + f32(x1[s, :, cols(n)])
                proj[s, rows64(keep), cols(n)] = total.astype(jnp.bfloat16)
                x_2(s, n).start()

    def stage_d(s):
        @pl.when(is_dest(s))
        def _():
            keep = 1 - sent_half(s)

            @pl.loop(0, CHUNKS)
            def _(n):
                wait_into(x1.at[s, :, cols(n)], x1_recv.at[s, n])
                wait_into(x2.at[s, :, cols(n)], x2_recv.at[s, n])
                g = 1 - zh
                total = f32(proj[s, rows32(keep, g), cols(n)])
                total += f32(x1[s, rows32(0, g), cols(n)]) + f32(x2[s, rows32(0, g), cols(n)])
                zout[s, :, cols(n)] = total.astype(jnp.bfloat16)
                z_h(s, n).start()

    def fin_copy():
        return remote(done, fin, fin_send, fin_recv, pool=here)

    def stage_e(s):
        @pl.when(is_dest(s))
        def _():
            keep = 1 - sent_half(s)
            mine = owner(s) == core

            def total(n):
                wait_into(zin.at[s, :, cols(n)], zh_recv.at[s, n])
                t = f32(proj[s, rows32(keep, zh), cols(n)]) + f32(zin[s, :, cols(n)])
                return t + f32(x1[s, rows32(0, zh), cols(n)]) + f32(x2[s, rows32(0, zh), cols(n)])

            def at(n):
                return pl.ds(pl.multiple_of(core * width + n * chunk, chunk), chunk)

            @pl.when(mine)
            def _():
                @pl.loop(0, CHUNKS)
                def _(n):
                    out_ref[:, at(n)] = (total(n) + f32(res_ref[:, at(n)])).astype(jnp.bfloat16)

            @pl.when(jnp.logical_not(mine))
            def _():
                wait_into(res_sib, kv_recv.at[3])

                @pl.loop(0, CHUNKS)
                def _(n):
                    done[:, cols(n)] = (total(n) + f32(res_sib[:, cols(n)])).astype(jnp.bfloat16)

                fin_copy().start()

    nk_own.wait()
    for copy in (k_copy, nk_copy, v_copy, res_copy):
        copy.wait_send()
    wait_into(nkv.at[sib], kv_recv.at[0])
    wait_into(k_sib, kv_recv.at[1])
    wait_into(vt_sib, kv_recv.at[2])

    @pl.loop(0, SLOTS + 5)
    def _(t):
        def stage(f, s):
            @pl.when(jnp.logical_and(s >= 0, s < SLOTS))
            def _():
                f(s)

        stage(stage_c, t)
        stage(stage_h, t - 1)

        @pl.when(t + 1 < SLOTS)
        def _():
            @pl.when(t >= 1)
            def _():
                for z in others:
                    z_arrived(t + 1, z)

            stage_r(t + 1)

        stage(stage_m, t)
        stage(stage_x, t - 3)
        stage(stage_d, t - 4)
        stage(stage_e, t - 5)
        stage(stage_o, t - 2)
        stage(stage_f, t - 1)

    for j in range(2):
        for k in range(NZ - 1):
            for c in range(2):
                q_z(j, k, c).wait_send()
        q_sib(j).wait_send()

    @pl.loop(0, SLOTS)
    def _(s):
        for d in range(2):
            for z in range(NZ):
                q_y(s, d, z).wait_send()
                p_1(s, d, z).wait_send()
            for j in range(2):
                q_relay(s, d, j).wait_send()
                p_2(s, d, j).wait_send()
        for z in others:
            p_z(s, z).wait_send()
        a_copy(s).wait_send()
        for n in range(CHUNKS):
            x_1(s, n).wait_send()

            @pl.when(is_dest(s))
            def _():
                z_h(s, n).wait_send()

            @pl.when(jnp.logical_not(is_dest(s)))
            def _():
                x_2(s, n).wait_send()

    fin_copy().wait_send()
    wait_into(fin, fin_recv)
    out_ref[:, columns(sib)] = fin[...]


def layer(tab, queries, nkv, store, residual, weight):
    bf = jnp.bfloat16
    blocks = store.shape[0]
    depth, width = weight.shape[0], weight.shape[1] // 2
    rows = residual.shape[0]
    vmem = pl.BlockSpec(memory_space=pltpu.VMEM)
    dma = pltpu.SemaphoreType.DMA
    unit = (ROWS, 2 * NEW)
    each = [dma((SLOTS, CHUNKS))] * 2
    return pl.pallas_call(
        layer_kernel,
        out_shape=jax.ShapeDtypeStruct(residual.shape, bf),
        in_specs=[pl.BlockSpec(memory_space=pltpu.SMEM)] + [vmem] * 4 + [pl.BlockSpec(memory_space=pl.ANY)],
        out_specs=vmem,
        scratch_shapes=[
            pltpu.VMEM((SLOTS, NY, NZ, NEW, 2 * HEAD), bf),
            pltpu.VMEM((blocks, BLOCK, HEAD), bf),
            pltpu.VMEM((blocks, HEAD, BLOCK), bf),
            pltpu.VMEM((blocks, HEAD, BLOCK), bf),
            pltpu.VMEM((2, 2 * NEW, 2 * HEAD), bf),
            pltpu.VMEM((SLOTS, NY, NZ) + unit, bf),
            pltpu.VMEM((SLOTS, 2, 2) + unit, bf),
            pltpu.VMEM((SLOTS, 2, NZ) + unit, bf),
            pltpu.VMEM((SLOTS, NZ) + unit, bf),
            pltpu.VMEM((SLOTS, NEW, 4 * HEAD), bf),
            pltpu.VMEM((depth, width), bf),
            pltpu.VMEM((rows, width), bf),
            pltpu.VMEM((SLOTS, NEW, width), bf),
            pltpu.VMEM((SLOTS, NEW // 2, width), bf),
            pltpu.VMEM((SLOTS, NEW // 2, width), bf),
            pltpu.VMEM((SLOTS, NEW // 4, width), bf),
            pltpu.VMEM((SLOTS, NEW // 4, width), bf),
            pltpu.VMEM((rows, width), bf),
            pltpu.VMEM((rows, width), bf),
            dma((4,)), dma((4,)), dma((2,)),
            dma((2, NZ, 2)), dma((SLOTS, NZ)),
            dma((SLOTS, 2, NZ)), dma((SLOTS, 2, NZ)), dma((SLOTS, 2, 2)), dma((SLOTS, 2, 2)),
            dma((SLOTS, 2, 2)), dma((SLOTS, 2, 2)), dma((SLOTS, 2, NZ)), dma((SLOTS, 2, NZ)),
            dma((SLOTS, NZ)), dma((SLOTS, NZ)), dma((SLOTS,)), dma((SLOTS,)),
            *each, *each, *each, dma(()), dma(()),
        ],
        compiler_params=pltpu.CompilerParams(
            collective_id=0, has_side_effects=True, vmem_limit_bytes=56 * 1024 * 1024
        ),
    )(tab, queries, nkv, store, residual, weight)


def hit_table(hit_dev, hit_blk, prefix_len):
    me = lax.axis_index("pool")
    start = jnp.arange(MAXB, dtype=jnp.int32) * BLOCK
    count = jnp.clip(prefix_len[:, None] - start[None, :], 0, BLOCK)
    code = hit_blk + 32 * count
    return jnp.stack([jnp.sum(jnp.where(hit_dev == d, code, 0), axis=1) for d in (me, me + 1 - 2 * (me % 2))])


def shards(queries, new_key_values, key_value_store, o_weight, residual, hit_dev, hit_blk, prefix_len):
    tab = hit_table(hit_dev, hit_blk, prefix_len)
    return layer(tab, queries, new_key_values, key_value_store, residual, o_weight)


def solution(mesh):
    placed = (
        P("pool", "tp"),
        P("pool", "tp"),
        P("pool", None, "tp"),
        P("tp", None),
        P(("pool", "tp"), None),
        P(),
        P(),
        P(),
    )
    return jax.shard_map(
        shards, mesh=mesh, in_specs=placed, out_specs=P(("pool", "tp"), None), check_vma=False
    )
```

time: 266 us -> 152 us (0.57)
  waiting for transfers between devices: 126 us -> 0 us
  Pallas kernels: 110 us -> 148 us
  between operations: 13.4 us -> 0.01 us
  matrix products: 7.72 us -> 0 us
    reduce_scatter x1 -> x0, waiting for transfers between devices: 126 us -> none  [shards(): lax.psum_scatter(jnp.dot(attn, o_weight, preferred_element_type=jnp.float...]
    pallas_call x1, Pallas kernels: 110 us -> 148 us  [layer(): pl.pallas_call(layer_kernel, out_shape=jax.ShapeDtypeStruct(residual.shap...]
    dot_general x1 -> x0, matrix products: 7.72 us -> none  [shards(): jnp.dot(attn, o_weight, preferred_element_type=jnp.float32)]
  transfers between devices with their start and end apart: 1 -> 0, of which waited for: 1 -> 0; matrix products, arithmetic and copies ran while one was open for 0% -> 0% of each run, Pallas kernels for 0% -> 0%
where the time goes in v2:
time: 152 us; the launch traced here: 151 us
  Pallas kernels  148 us (97%)
  local copies, waits for them, and re-layouts  1.87 us (1%)
    pallas_call x1, Pallas kernels, layer(): pl.pallas_call(layer_kernel, out_shape=jax.ShapeDtypeStruct(residual.shap...  148 us

profile of v2, /device:TPU:4, one launch (start us, length us, event | category | flops | bytes accessed | tf_op | source)
XLA Modules:
  0.0 151.5 jit_solution(14633773019947860829)
XLA Ops:
  0.0 0.8 select_reduce_fusion.1
  0.8 0.6 pad_add_fusion.tab
  1.4 148.2 %shard_map.82 = bf16[32,8192]{1,0:T(8,128)(2,1)} custom-call(s32[2,64]{1,0:T(2,128)} %pad_add_fusion.tab, bf16[256,512]{1,0:T(8,128)(2,1)} %q_ref.1, bf16[256,256]{1,0:T(8,128)(2,1)} %nkv_ref.1, bf16[24,256,256]{2,1,0:T(8,128)(2,1)} %kv_ref.1, bf16[32,8192]{1,0:T(8,128)(2,1)} %res_ref.1, bf16[512,8192]{1,0:T(8,128)(2,1)} %w_ref.1), custom_call_target="tpu_custom_call" | custom-call | tf_op jit(solution)/shard_map/pallas_call | solution.py:494
  149.6 1.9 %copy.10 = bf16[32,8192]{1,0:T(8,128)(2,1)} copy(bf16[32,8192]{1,0:T(8,128)(2,1)} %shard_map.82) | data formatting | bytes 1048576
  (1 shorter events, 0.0 us)

commit v3 on v2

--- a/solution.py
+++ b/solution.py
@@ -15,8 +15,9 @@
 NY = 4
 NZ = 4
 NX = 4
-SLOTS = 4
-CHUNKS = 2
+PART = 16
+SLOTS = 8
+CHUNKS = 4
 LOG2_SCALE = HEAD**-0.5 * math.log2(math.e)
 FLOOR = -1e30
 ROWS = 144
@@ -27,14 +28,10 @@
     return lax.dot_general(a, b, (((1,), (1,)), ((), ())), preferred_element_type=jnp.float32)
 
 
-def stacked(q):
-    return jnp.concatenate([q[:, :HEAD], q[:, HEAD:]], axis=0)
-
-
 def put(ref, at, o, m, l):
     ref[at + (slice(0, HEAD), slice(None))] = o.astype(jnp.bfloat16)
     high = l.astype(jnp.bfloat16).astype(jnp.float32)
-    row = lax.broadcasted_iota(jnp.int32, (16, 2 * NEW), 0)
+    row = lax.broadcasted_iota(jnp.int32, (16, NEW), 0)
     stats = jnp.where(row == 0, m, jnp.where(row == 1, high, jnp.where(row == 2, l - high, 0.0)))
     ref[at + (slice(HEAD, ROWS), slice(None))] = stats.astype(jnp.bfloat16)
 
@@ -55,14 +52,16 @@
 
 
 def layer_kernel(
-    tab, q_ref, nkv_ref, kv_ref, res_ref, w_ref, out_ref,
-    qbuf, k_sib, vt_own, vt_sib, nkv, part, r2, r1, rz, att,
+    tab, q_ref, nkv_ref, res_ref, store_ref, w_ref, out_ref,
+    kv_ref, qsrc, qbuf, k_sib, vt_own, vt_sib, nkv, part, r2, r1, rz, att,
     w, res_sib, proj, x1, x2, zout, zin, done, fin,
     kv_send, kv_recv, local,
     qz_send, qz_recv, qy_send, qy_recv, qr_send, qr_recv,
     p2_send, p2_recv, p1_send, p1_recv, pz_send, pz_recv, at_send, at_recv,
     x1_send, x1_recv, x2_send, x2_recv, zh_send, zh_recv, fin_send, fin_recv,
 ):
+    kv_own = pltpu.make_async_copy(store_ref, kv_ref, local.at[2])
+    kv_own.start()
     me, tp = lax.axis_index("pool"), lax.axis_index("tp")
     core = lax.rem(me, 2)
     mz = lax.rem(lax.div(me, 2), NZ)
@@ -97,6 +96,14 @@
     partners += [{"tp": p} for p in (tp_of(pair, zh), tp_of(facing, zh), tp_of(mx, 1 - zh))]
     for p in partners:
         pl.semaphore_signal(barrier, inc=1, device_id=p, device_id_type=MESH)
+
+    for i in range(2):
+        for g in range(2):
+            for h in range(4):
+                for b in range(4):
+                    to, at = (h % 2 * 4 + b) * PART, i * NEW + (2 * b + g) * PART
+                    qsrc[i, g, h // 2, to : to + PART, :] = q_ref[at : at + PART, h * HEAD : (h + 1) * HEAD]
+
     pl.semaphore_wait(barrier, len(partners))
 
     def half(c):
@@ -106,30 +113,34 @@
         return pl.ds(pl.multiple_of(c * width, width), width)
 
     def owner(s):
-        return lax.rem(s + lax.div(s, 2), 2)
-
-    firsts = ((core, core), (sib, 2 + sib))
+        return lax.rem(s, 2)
+
+    def which(s):
+        return lax.rem(lax.div(s, 2) + lax.rem(s, 2), 2)
+
+    def share(s):
+        return lax.div(s, 4)
 
     def tokens(i):
         return pl.ds(pl.multiple_of(i * NEW, NEW), NEW)
 
     def q_z(j, k, c):
-        i, s = firsts[j]
-        return remote(
-            q_ref.at[tokens(i), half(c)], qbuf.at[s, my, mz],
+        s = 2 * j + core
+        return remote(
+            qsrc.at[which(s), lax.div(j, 2), c], qbuf.at[s, my, mz],
             qz_send.at[j, k, c], qz_recv.at[s, mz], pool=dev(my, others[k], c),
         )
 
     def q_sib(j):
-        i, s = firsts[j]
-        return remote(
-            q_ref.at[tokens(i), half(sib)], qbuf.at[s, my, mz],
+        s = 2 * j + core
+        return remote(
+            qsrc.at[which(s), j // 2, sib], qbuf.at[s, my, mz],
             qz_send.at[j, 3, 0], qz_recv.at[s, mz], pool=dev(my, mz, sib),
         )
 
     def q_own(j):
-        i, s = firsts[j]
-        return pltpu.make_async_copy(q_ref.at[tokens(i), half(core)], qbuf.at[s, my, mz], qz_recv.at[s, mz])
+        s = 2 * j + core
+        return pltpu.make_async_copy(qsrc.at[which(s), j // 2, core], qbuf.at[s, my, mz], qz_recv.at[s, mz])
 
     here = dev(my, mz, sib)
     nk_copy = remote(nkv_ref, nkv.at[core], kv_send.at[0], kv_recv.at[0], pool=here)
@@ -156,22 +167,32 @@
     def y_arrived(s, d, z):
         wait_into(qbuf.at[s, (down, up)[d], z], qy_recv.at[s, d, z])
 
+    def relay_two(s, j):
+        for d in range(2):
+            y_arrived(s, d, 2 * d + j)
+            q_relay(s, d, j).start()
+
     def stage_r(s):
         for j in range(2):
-            for d in range(2):
-                y_arrived(s, d, 2 * d + j)
-                q_relay(s, d, j).start()
-
-    for j in range(2):
+            relay_two(s, j)
+
+    per_core = SLOTS // 2
+
+    def send_z(j):
+        for k in range(NZ - 1):
+            for c in range(2):
+                q_z(j, k, c).start()
+
+    for j in range(per_core):
         q_own(j).start()
         q_sib(j).start()
-    for k in range(NZ - 1):
-        for c in range(2):
-            q_z(0, k, c).start()
-    for s in range(2):
+        if j == 0:
+            send_z(0)
+    for s in range(4):
         z_arrived(s, mz)
     nk_own.start()
     nk_copy.start()
+    kv_own.wait()
     k_copy.start()
 
     @pl.loop(0, kv_ref.shape[0])
@@ -180,22 +201,18 @@
 
     v_copy.start()
     for z in others:
-        for s in range(2):
-            z_arrived(s, z)
-    for k in range(NZ - 1):
-        for c in range(2):
-            q_z(1, k, c).start()
-    for s in range(2):
-        z_arrived(2 + s, mz)
+        z_arrived(0, z)
+        z_arrived(1, z)
+    send_z(1)
     res_copy.start()
     w_own.start()
     stage_r(0)
 
-    key = lax.broadcasted_iota(jnp.int32, (BLOCK, 2 * NEW), 0)
+    key = lax.broadcasted_iota(jnp.int32, (BLOCK, NEW), 0)
 
     def attend(s, y, z):
-        r = dev(y, z, owner(s)) * 2 + lax.rem(s, 2)
-        q = stacked(qbuf[s, y, z])
+        r = dev(y, z, owner(s)) * 2 + which(s)
+        q = qbuf[s, y, z]
         codes = [tab[0, r], tab[1, r]]
         blocks = [c % 32 for c in codes]
         counts = [c // 32 for c in codes]
@@ -235,24 +252,37 @@
                 wait_into(qbuf.at[s, across, 2 * d + j], qr_recv.at[s, d, j])
                 y_arrived(s, d, 2 - 2 * d + j)
 
-        @pl.loop(0, 2)
-        def _(j):
-            attend(s, across, j)
-            attend(s, across, 2 + j)
+        for z in range(NZ):
+            attend(s, across, z)
+        for j in range(2):
             p_2(s, 0, j).start()
             p_2(s, 1, j).start()
 
-        @pl.loop(0, 2)
-        def _(j):
+        @pl.when(s == 0)
+        def _():
+            for z in others:
+                z_arrived(2, z)
+
+        for j in range(2):
             attend(s, up, 2 + j)
             attend(s, down, j)
+        for j in range(2):
             p_1(s, 0, 2 + j).start()
             p_1(s, 1, j).start()
 
-        @pl.loop(0, 2)
-        def _(j):
+        @pl.when(s == 0)
+        def _():
+            stage_r(1)
+
+        for j in range(2):
             attend(s, up, j)
             attend(s, down, 2 + j)
+        for z in range(NZ):
+            attend(s, my, z)
+
+        @pl.when(s + 2 < SLOTS)
+        def _():
+            stage_r(s + 2)
 
     def stage_m(s):
         @pl.loop(0, 2)
@@ -263,10 +293,18 @@
                 put(part, (s, to, z), *merge([get(part, (s, to, z)), get(r2, (s, d, j))]))
                 p_1(s, d, z).start()
 
-        @pl.loop(0, 2)
-        def _(j):
-            attend(s, my, j)
-            attend(s, my, 2 + j)
+        @pl.when(s + 4 < SLOTS)
+        def _():
+            z_arrived(s + 4, mz)
+
+        @pl.when(s + 3 < SLOTS)
+        def _():
+            for z in others:
+                z_arrived(s + 3, z)
+
+        @pl.when(jnp.logical_or(s == 0, s == 2))
+        def _():
+            send_z(lax.div(s, 2) + 2)
 
     def stage_h(s):
         @pl.loop(0, NZ)
@@ -281,10 +319,11 @@
                 p_z(s, z).start()
 
     def fresh(s):
-        q = stacked(qbuf[s, my, mz])
-        rows = nkv[owner(s), tokens(lax.rem(s, 2)), :]
-        j = lax.broadcasted_iota(jnp.int32, (NEW, 2 * NEW), 0)
-        i = lax.broadcasted_iota(jnp.int32, (NEW, 2 * NEW), 1) % NEW
+        q = qbuf[s, my, mz]
+        rows = nkv[owner(s), tokens(which(s)), :]
+        j = lax.broadcasted_iota(jnp.int32, (NEW, NEW), 0)
+        i = lax.broadcasted_iota(jnp.int32, (NEW, NEW), 1) % (4 * PART)
+        i = i + i // PART * PART + share(s) * PART
         t = jnp.where(j <= i, nt(rows[:, :HEAD], q) * LOG2_SCALE, -jnp.inf)
         m = jnp.max(t, axis=0, keepdims=True).astype(jnp.bfloat16).astype(jnp.float32)
         e = jnp.exp2(t - m)
@@ -302,33 +341,34 @@
             parts.append(get(rz, (s, z)))
         o, _, l = merge(parts)
         o = o / l
-        att[s, :, half(core)] = jnp.concatenate([o[:, :NEW].T, o[:, NEW:].T], axis=1).astype(jnp.bfloat16)
+        o = o.T
+        att[s, :, half(core)] = jnp.concatenate([o[: 4 * PART], o[4 * PART :]], axis=1).astype(jnp.bfloat16)
         a_copy(s).start()
 
     def is_dest(s):
-        return lax.div(mx, 2) == lax.rem(s, 2)
+        return lax.div(mx, 2) == which(s)
 
     def sent_half(s):
         return jnp.where(is_dest(s), 1 - lax.rem(mx, 2), lax.rem(mx, 2))
 
-    def rows64(h):
-        return pl.ds(pl.multiple_of(h * 64, 64), 64)
-
-    def rows32(h, g):
-        return pl.ds(pl.multiple_of(h * 64 + g * 32, 32), 32)
+    def rows(h):
+        return pl.ds(pl.multiple_of(h * 2 * PART, 2 * PART), 2 * PART)
+
+    def part_of(h, z):
+        return pl.ds(pl.multiple_of((2 * h + z) * PART, PART), PART)
 
     def cols(n):
         return pl.ds(pl.multiple_of(n * chunk, chunk), chunk)
 
     def x_1(s, n):
         return remote(
-            proj.at[s, rows64(sent_half(s)), cols(n)], x1.at[s, :, cols(n)],
+            proj.at[s, rows(sent_half(s)), cols(n)], x1.at[s, :, cols(n)],
             x1_send.at[s, n], x1_recv.at[s, n], tp=tp_of(pair, zh),
         )
 
     def x_2(s, n):
         return remote(
-            proj.at[s, rows64(1 - sent_half(s)), cols(n)], x2.at[s, :, cols(n)],
+            proj.at[s, rows(1 - sent_half(s)), cols(n)], x2.at[s, :, cols(n)],
             x2_send.at[s, n], x2_recv.at[s, n], tp=tp_of(facing, zh),
         )
 
@@ -363,8 +403,8 @@
             @pl.loop(0, CHUNKS)
             def _(n):
                 wait_into(x1.at[s, :, cols(n)], x1_recv.at[s, n])
-                total = f32(proj[s, rows64(keep), cols(n)]) + f32(x1[s, :, cols(n)])
-                proj[s, rows64(keep), cols(n)] = total.astype(jnp.bfloat16)
+                total = f32(proj[s, rows(keep), cols(n)]) + f32(x1[s, :, cols(n)])
+                proj[s, rows(keep), cols(n)] = total.astype(jnp.bfloat16)
                 x_2(s, n).start()
 
     def stage_d(s):
@@ -376,25 +416,27 @@
             def _(n):
                 wait_into(x1.at[s, :, cols(n)], x1_recv.at[s, n])
                 wait_into(x2.at[s, :, cols(n)], x2_recv.at[s, n])
-                g = 1 - zh
-                total = f32(proj[s, rows32(keep, g), cols(n)])
-                total += f32(x1[s, rows32(0, g), cols(n)]) + f32(x2[s, rows32(0, g), cols(n)])
+                z = 1 - zh
+                total = f32(proj[s, part_of(keep, z), cols(n)])
+                total += f32(x1[s, part_of(0, z), cols(n)]) + f32(x2[s, part_of(0, z), cols(n)])
                 zout[s, :, cols(n)] = total.astype(jnp.bfloat16)
                 z_h(s, n).start()
 
-    def fin_copy():
-        return remote(done, fin, fin_send, fin_recv, pool=here)
+    def fin_copy(g):
+        return remote(done.at[g], fin.at[g], fin_send.at[g], fin_recv.at[g], pool=here)
 
     def stage_e(s):
         @pl.when(is_dest(s))
         def _():
             keep = 1 - sent_half(s)
             mine = owner(s) == core
+            g = share(s)
+            out_rows = pl.ds(pl.multiple_of(g * PART, PART), PART)
 
             def total(n):
                 wait_into(zin.at[s, :, cols(n)], zh_recv.at[s, n])
-                t = f32(proj[s, rows32(keep, zh), cols(n)]) + f32(zin[s, :, cols(n)])
-                return t + f32(x1[s, rows32(0, zh), cols(n)]) + f32(x2[s, rows32(0, zh), cols(n)])
+                t = f32(proj[s, part_of(keep, zh), cols(n)]) + f32(zin[s, :, cols(n)])
+                return t + f32(x1[s, part_of(0, zh), cols(n)]) + f32(x2[s, part_of(0, zh), cols(n)])
 
             def at(n):
                 return pl.ds(pl.multiple_of(core * width + n * chunk, chunk), chunk)
@@ -403,17 +445,15 @@
             def _():
                 @pl.loop(0, CHUNKS)
                 def _(n):
-                    out_ref[:, at(n)] = (total(n) + f32(res_ref[:, at(n)])).astype(jnp.bfloat16)
+                    out_ref[out_rows, at(n)] = (total(n) + f32(res_ref[out_rows, at(n)])).astype(jnp.bfloat16)
 
             @pl.when(jnp.logical_not(mine))
             def _():
-                wait_into(res_sib, kv_recv.at[3])
-
                 @pl.loop(0, CHUNKS)
                 def _(n):
-                    done[:, cols(n)] = (total(n) + f32(res_sib[:, cols(n)])).astype(jnp.bfloat16)
-
-                fin_copy().start()
+                    done[g, :, cols(n)] = (total(n) + f32(res_sib[out_rows, cols(n)])).astype(jnp.bfloat16)
+
+                fin_copy(g).start()
 
     nk_own.wait()
     for copy in (k_copy, nk_copy, v_copy, res_copy):
@@ -421,8 +461,9 @@
     wait_into(nkv.at[sib], kv_recv.at[0])
     wait_into(k_sib, kv_recv.at[1])
     wait_into(vt_sib, kv_recv.at[2])
-
-    @pl.loop(0, SLOTS + 5)
+    wait_into(res_sib, kv_recv.at[3])
+
+    @pl.loop(0, SLOTS + 2)
     def _(t):
         def stage(f, s):
             @pl.when(jnp.logical_and(s >= 0, s < SLOTS))
@@ -431,24 +472,21 @@
 
         stage(stage_c, t)
         stage(stage_h, t - 1)
-
-        @pl.when(t + 1 < SLOTS)
-        def _():
-            @pl.when(t >= 1)
-            def _():
-                for z in others:
-                    z_arrived(t + 1, z)
-
-            stage_r(t + 1)
-
+        stage(stage_f, t - 2)
         stage(stage_m, t)
+        stage(stage_d, t - 5)
+        stage(stage_o, t - 2)
         stage(stage_x, t - 3)
-        stage(stage_d, t - 4)
-        stage(stage_e, t - 5)
-        stage(stage_o, t - 2)
-        stage(stage_f, t - 1)
-
-    for j in range(2):
+
+    stage_x(SLOTS - 1)
+    for s in range(SLOTS - 3, SLOTS):
+        stage_d(s)
+
+    @pl.loop(0, SLOTS)
+    def _(s):
+        stage_e(s)
+
+    for j in range(per_core):
         for k in range(NZ - 1):
             for c in range(2):
                 q_z(j, k, c).wait_send()
@@ -477,9 +515,10 @@
             def _():
                 x_2(s, n).wait_send()
 
-    fin_copy().wait_send()
-    wait_into(fin, fin_recv)
-    out_ref[:, columns(sib)] = fin[...]
+    for g in range(2):
+        fin_copy(g).wait_send()
+        wait_into(fin.at[g], fin_recv.at[g])
+        out_ref[g * PART : (g + 1) * PART, columns(sib)] = fin[g]
 
 
 def layer(tab, queries, nkv, store, residual, weight):
@@ -489,15 +528,17 @@
     rows = residual.shape[0]
     vmem = pl.BlockSpec(memory_space=pltpu.VMEM)
     dma = pltpu.SemaphoreType.DMA
-    unit = (ROWS, 2 * NEW)
+    unit = (ROWS, NEW)
     each = [dma((SLOTS, CHUNKS))] * 2
     return pl.pallas_call(
         layer_kernel,
         out_shape=jax.ShapeDtypeStruct(residual.shape, bf),
-        in_specs=[pl.BlockSpec(memory_space=pltpu.SMEM)] + [vmem] * 4 + [pl.BlockSpec(memory_space=pl.ANY)],
+        in_specs=[pl.BlockSpec(memory_space=pltpu.SMEM)] + [vmem] * 3 + [pl.BlockSpec(memory_space=pl.ANY)] * 2,
         out_specs=vmem,
         scratch_shapes=[
-            pltpu.VMEM((SLOTS, NY, NZ, NEW, 2 * HEAD), bf),
+            pltpu.VMEM(store.shape, bf),
+            pltpu.VMEM((2, 2, 2, NEW, HEAD), bf),
+            pltpu.VMEM((SLOTS, NY, NZ, NEW, HEAD), bf),
             pltpu.VMEM((blocks, BLOCK, HEAD), bf),
             pltpu.VMEM((blocks, HEAD, BLOCK), bf),
             pltpu.VMEM((blocks, HEAD, BLOCK), bf),
@@ -506,27 +547,27 @@
             pltpu.VMEM((SLOTS, 2, 2) + unit, bf),
             pltpu.VMEM((SLOTS, 2, NZ) + unit, bf),
             pltpu.VMEM((SLOTS, NZ) + unit, bf),
-            pltpu.VMEM((SLOTS, NEW, 4 * HEAD), bf),
+            pltpu.VMEM((SLOTS, 4 * PART, 4 * HEAD), bf),
             pltpu.VMEM((depth, width), bf),
             pltpu.VMEM((rows, width), bf),
-            pltpu.VMEM((SLOTS, NEW, width), bf),
-            pltpu.VMEM((SLOTS, NEW // 2, width), bf),
-            pltpu.VMEM((SLOTS, NEW // 2, width), bf),
-            pltpu.VMEM((SLOTS, NEW // 4, width), bf),
-            pltpu.VMEM((SLOTS, NEW // 4, width), bf),
-            pltpu.VMEM((rows, width), bf),
-            pltpu.VMEM((rows, width), bf),
-            dma((4,)), dma((4,)), dma((2,)),
-            dma((2, NZ, 2)), dma((SLOTS, NZ)),
+            pltpu.VMEM((SLOTS, 4 * PART, width), bf),
+            pltpu.VMEM((SLOTS, 2 * PART, width), bf),
+            pltpu.VMEM((SLOTS, 2 * PART, width), bf),
+            pltpu.VMEM((SLOTS, PART, width), bf),
+            pltpu.VMEM((SLOTS, PART, width), bf),
+            pltpu.VMEM((2, PART, width), bf),
+            pltpu.VMEM((2, PART, width), bf),
+            dma((4,)), dma((4,)), dma((3,)),
+            dma((SLOTS // 2, NZ, 2)), dma((SLOTS, NZ)),
             dma((SLOTS, 2, NZ)), dma((SLOTS, 2, NZ)), dma((SLOTS, 2, 2)), dma((SLOTS, 2, 2)),
             dma((SLOTS, 2, 2)), dma((SLOTS, 2, 2)), dma((SLOTS, 2, NZ)), dma((SLOTS, 2, NZ)),
             dma((SLOTS, NZ)), dma((SLOTS, NZ)), dma((SLOTS,)), dma((SLOTS,)),
-            *each, *each, *each, dma(()), dma(()),
+            *each, *each, *each, dma((2,)), dma((2,)),
         ],
         compiler_params=pltpu.CompilerParams(
             collective_id=0, has_side_effects=True, vmem_limit_bytes=56 * 1024 * 1024
         ),
-    )(tab, queries, nkv, store, residual, weight)
+    )(tab, queries, nkv, residual, store, weight)
 
 
 def hit_table(hit_dev, hit_blk, prefix_len):

time: 152 us -> 143 us (0.941)
  Pallas kernels: 148 us -> 138 us
    pallas_call x1, Pallas kernels: 148 us -> 138 us  [layer(): pl.pallas_call(layer_kernel, out_shape=jax.ShapeDtypeStruct(residual.shap...]
where the time goes in v3:
time: 143 us; the launch traced here: 142 us
  Pallas kernels  138 us (97%)
  local copies, waits for them, and re-layouts  1.87 us (1%)
    pallas_call x1, Pallas kernels, layer(): pl.pallas_call(layer_kernel, out_shape=jax.ShapeDtypeStruct(residual.shap...  138 us

profile of v3, /device:TPU:4, one launch (start us, length us, event | category | flops | bytes accessed | tf_op | source)
XLA Modules:
  0.0 141.7 jit_solution(1925650042023314244)
XLA Ops:
  0.0 0.8 select_reduce_fusion.1
  0.8 0.6 pad_add_fusion.tab
  1.4 138.4 %shard_map.82 = bf16[32,8192]{1,0:T(8,128)(2,1)} custom-call(s32[2,64]{1,0:T(2,128)} %pad_add_fusion.tab, bf16[256,512]{1,0:T(8,128)(2,1)} %q_ref.1, bf16[256,256]{1,0:T(8,128)(2,1)} %nkv_ref.1, bf16[32,8192]{1,0:T(8,128)(2,1)} %res_ref.1, bf16[24,256,256]{2,1,0:T(8,128)(2,1)} %store_ref.1, bf16[512,8192]{1,0:T(8,128)(2,1)} %w_ref.1), custom_call_target="tpu_custom_call" | custom-call | tf_op jit(solution)/shard_map/pallas_call | solution.py:533
  139.8 1.9 %copy.10 = bf16[32,8192]{1,0:T(8,128)(2,1)} copy(bf16[32,8192]{1,0:T(8,128)(2,1)} %shard_map.82) | data formatting | bytes 1048576
  (1 shorter events, 0.0 us)

commit v4 on v3

--- a/solution.py
+++ b/solution.py
@@ -56,7 +56,7 @@
     kv_ref, qsrc, qbuf, k_sib, vt_own, vt_sib, nkv, part, r2, r1, rz, att,
     w, res_sib, proj, x1, x2, zout, zin, done, fin,
     kv_send, kv_recv, local,
-    qz_send, qz_recv, qy_send, qy_recv, qr_send, qr_recv,
+    qs_send, qz_send, qz_recv, qy_send, qy_recv, qr_send, qr_recv,
     p2_send, p2_recv, p1_send, p1_recv, pz_send, pz_recv, at_send, at_recv,
     x1_send, x1_recv, x2_send, x2_recv, zh_send, zh_recv, fin_send, fin_recv,
 ):
@@ -128,14 +128,14 @@
         s = 2 * j + core
         return remote(
             qsrc.at[which(s), lax.div(j, 2), c], qbuf.at[s, my, mz],
-            qz_send.at[j, k, c], qz_recv.at[s, mz], pool=dev(my, others[k], c),
+            qz_send, qz_recv.at[s, mz], pool=dev(my, others[k], c),
         )
 
     def q_sib(j):
         s = 2 * j + core
         return remote(
             qsrc.at[which(s), j // 2, sib], qbuf.at[s, my, mz],
-            qz_send.at[j, 3, 0], qz_recv.at[s, mz], pool=dev(my, mz, sib),
+            qs_send, qz_recv.at[s, mz], pool=dev(my, mz, sib),
         )
 
     def q_own(j):
@@ -152,12 +152,12 @@
 
     def q_y(s, d, z):
         piece = qbuf.at[s, my, z]
-        return remote(piece, piece, qy_send.at[s, d, z], qy_recv.at[s, d, z], pool=dev((up, down)[d], mz, core))
+        return remote(piece, piece, qy_send, qy_recv.at[s, d, z], pool=dev((up, down)[d], mz, core))
 
     def q_relay(s, d, j):
         to, of = ((up, down), (down, up))[d]
         piece = qbuf.at[s, of, 2 * d + j]
-        return remote(piece, piece, qr_send.at[s, d, j], qr_recv.at[s, d, j], pool=dev(to, mz, core))
+        return remote(piece, piece, qr_send, qr_recv.at[s, d, j], pool=dev(to, mz, core))
 
     def z_arrived(s, z):
         wait_into(qbuf.at[s, my, z], qz_recv.at[s, z])
@@ -232,18 +232,18 @@
     def p_2(s, d, j):
         return remote(
             part.at[s, across, 2 * d + j], r2.at[s, d, j],
-            p2_send.at[s, d, j], p2_recv.at[s, d, j], pool=dev((up, down)[d], mz, core),
+            p2_send, p2_recv.at[s, d, j], pool=dev((up, down)[d], mz, core),
         )
 
     def p_1(s, d, z):
         to = (up, down)[d]
         return remote(
-            part.at[s, to, z], r1.at[s, d, z], p1_send.at[s, d, z], p1_recv.at[s, d, z], pool=dev(to, mz, core)
+            part.at[s, to, z], r1.at[s, d, z], p1_send, p1_recv.at[s, d, z], pool=dev(to, mz, core)
         )
 
     def p_z(s, z):
         return remote(
-            part.at[s, my, z], rz.at[s, mz], pz_send.at[s, z], pz_recv.at[s, mz], pool=dev(my, z, core)
+            part.at[s, my, z], rz.at[s, mz], pz_send, pz_recv.at[s, mz], pool=dev(my, z, core)
         )
 
     def stage_c(s):
@@ -270,19 +270,15 @@
             p_1(s, 0, 2 + j).start()
             p_1(s, 1, j).start()
 
-        @pl.when(s == 0)
-        def _():
-            stage_r(1)
+        @pl.when(s + 1 < SLOTS)
+        def _():
+            stage_r(s + 1)
 
         for j in range(2):
             attend(s, up, j)
             attend(s, down, 2 + j)
         for z in range(NZ):
             attend(s, my, z)
-
-        @pl.when(s + 2 < SLOTS)
-        def _():
-            stage_r(s + 2)
 
     def stage_m(s):
         @pl.loop(0, 2)
@@ -332,7 +328,7 @@
 
     def a_copy(s):
         mine = att.at[s, :, half(core)]
-        return remote(mine, mine, at_send.at[s], at_recv.at[s], pool=here)
+        return remote(mine, mine, at_send, at_recv.at[s], pool=here)
 
     def stage_f(s):
         parts = [fresh(s), get(part, (s, my, mz))]
@@ -363,18 +359,18 @@
     def x_1(s, n):
         return remote(
             proj.at[s, rows(sent_half(s)), cols(n)], x1.at[s, :, cols(n)],
-            x1_send.at[s, n], x1_recv.at[s, n], tp=tp_of(pair, zh),
+            x1_send, x1_recv.at[s, n], tp=tp_of(pair, zh),
         )
 
     def x_2(s, n):
         return remote(
             proj.at[s, rows(1 - sent_half(s)), cols(n)], x2.at[s, :, cols(n)],
-            x2_send.at[s, n], x2_recv.at[s, n], tp=tp_of(facing, zh),
+            x2_send, x2_recv.at[s, n], tp=tp_of(facing, zh),
         )
 
     def z_h(s, n):
         return remote(
-            zout.at[s, :, cols(n)], zin.at[s, :, cols(n)], zh_send.at[s, n], zh_recv.at[s, n], tp=tp_of(mx, 1 - zh)
+            zout.at[s, :, cols(n)], zin.at[s, :, cols(n)], zh_send, zh_recv.at[s, n], tp=tp_of(mx, 1 - zh)
         )
 
     def stage_o(s):
@@ -423,7 +419,7 @@
                 z_h(s, n).start()
 
     def fin_copy(g):
-        return remote(done.at[g], fin.at[g], fin_send.at[g], fin_recv.at[g], pool=here)
+        return remote(done.at[g], fin.at[g], fin_send, fin_recv.at[g], pool=here)
 
     def stage_e(s):
         @pl.when(is_dest(s))
@@ -472,51 +468,37 @@
 
         stage(stage_c, t)
         stage(stage_h, t - 1)
+        stage(stage_m, t)
         stage(stage_f, t - 2)
-        stage(stage_m, t)
         stage(stage_d, t - 5)
         stage(stage_o, t - 2)
         stage(stage_x, t - 3)
+        stage(stage_e, t - 7)
 
     stage_x(SLOTS - 1)
     for s in range(SLOTS - 3, SLOTS):
         stage_d(s)
 
-    @pl.loop(0, SLOTS)
+    @pl.loop(SLOTS - 5, SLOTS)
     def _(s):
         stage_e(s)
 
-    for j in range(per_core):
-        for k in range(NZ - 1):
-            for c in range(2):
-                q_z(j, k, c).wait_send()
-        q_sib(j).wait_send()
-
-    @pl.loop(0, SLOTS)
-    def _(s):
-        for d in range(2):
-            for z in range(NZ):
-                q_y(s, d, z).wait_send()
-                p_1(s, d, z).wait_send()
-            for j in range(2):
-                q_relay(s, d, j).wait_send()
-                p_2(s, d, j).wait_send()
-        for z in others:
-            p_z(s, z).wait_send()
-        a_copy(s).wait_send()
-        for n in range(CHUNKS):
-            x_1(s, n).wait_send()
-
-            @pl.when(is_dest(s))
-            def _():
-                z_h(s, n).wait_send()
-
-            @pl.when(jnp.logical_not(is_dest(s)))
-            def _():
-                x_2(s, n).wait_send()
-
+    for ref, sem in (
+        (qbuf.at[pl.ds(0, 6), 0], qz_send),
+        (qbuf.at[0, 0], qs_send),
+        (qbuf.at[pl.ds(0, 4)], qy_send),
+        (qbuf.at[pl.ds(0, 2)], qr_send),
+        (part.at[pl.ds(0, 2)], p2_send),
+        (part.at[pl.ds(0, 4)], p1_send),
+        (part.at[pl.ds(0, 6), 0], pz_send),
+        (att.at[:, :, pl.ds(0, 2 * HEAD)], at_send),
+        (x1, x1_send),
+        (x2.at[pl.ds(0, SLOTS // 2)], x2_send),
+        (zout.at[pl.ds(0, SLOTS // 2)], zh_send),
+        (fin, fin_send),
+    ):
+        wait_into(ref, sem)
     for g in range(2):
-        fin_copy(g).wait_send()
         wait_into(fin.at[g], fin_recv.at[g])
         out_ref[g * PART : (g + 1) * PART, columns(sib)] = fin[g]
 
@@ -529,7 +511,7 @@
     vmem = pl.BlockSpec(memory_space=pltpu.VMEM)
     dma = pltpu.SemaphoreType.DMA
     unit = (ROWS, NEW)
-    each = [dma((SLOTS, CHUNKS))] * 2
+    one, each = dma(()), dma((SLOTS, CHUNKS))
     return pl.pallas_call(
         layer_kernel,
         out_shape=jax.ShapeDtypeStruct(residual.shape, bf),
@@ -558,11 +540,11 @@
             pltpu.VMEM((2, PART, width), bf),
             pltpu.VMEM((2, PART, width), bf),
             dma((4,)), dma((4,)), dma((3,)),
-            dma((SLOTS // 2, NZ, 2)), dma((SLOTS, NZ)),
-            dma((SLOTS, 2, NZ)), dma((SLOTS, 2, NZ)), dma((SLOTS, 2, 2)), dma((SLOTS, 2, 2)),
-            dma((SLOTS, 2, 2)), dma((SLOTS, 2, 2)), dma((SLOTS, 2, NZ)), dma((SLOTS, 2, NZ)),
-            dma((SLOTS, NZ)), dma((SLOTS, NZ)), dma((SLOTS,)), dma((SLOTS,)),
-            *each, *each, *each, dma((2,)), dma((2,)),
+            one, one, dma((SLOTS, NZ)),
+            one, dma((SLOTS, 2, NZ)), one, dma((SLOTS, 2, 2)),
+            one, dma((SLOTS, 2, 2)), one, dma((SLOTS, 2, NZ)),
+            one, dma((SLOTS, NZ)), one, dma((SLOTS,)),
+            one, each, one, each, one, each, one, dma((2,)),
         ],
         compiler_params=pltpu.CompilerParams(
             collective_id=0, has_side_effects=True, vmem_limit_bytes=56 * 1024 * 1024
@@ -572,10 +554,10 @@
 
 def hit_table(hit_dev, hit_blk, prefix_len):
     me = lax.axis_index("pool")
+    there = jnp.stack([me, me + 1 - 2 * (me % 2)])[:, None, None]
     start = jnp.arange(MAXB, dtype=jnp.int32) * BLOCK
     count = jnp.clip(prefix_len[:, None] - start[None, :], 0, BLOCK)
-    code = hit_blk + 32 * count
-    return jnp.stack([jnp.sum(jnp.where(hit_dev == d, code, 0), axis=1) for d in (me, me + 1 - 2 * (me % 2))])
+    return jnp.sum(jnp.where(hit_dev[None] == there, (hit_blk + 32 * count)[None], 0), axis=2)
 
 
 def shards(queries, new_key_values, key_value_store, o_weight, residual, hit_dev, hit_blk, prefix_len):

time: 143 us -> 141 us (0.986)
  the two profiles are of different devices: /device:TPU:4 before, /device:TPU:101 now
where the time goes in v4:
time: 141 us
  Pallas kernels  137 us (97%)
  other arithmetic  2.2 us (2%)
  local copies, waits for them, and re-layouts  1.87 us (1%)
    pallas_call x1, Pallas kernels, layer(): pl.pallas_call(layer_kernel, out_shape=jax.ShapeDtypeStruct(residual.shap...  137 us

profile of v4, /device:TPU:101, one launch (start us, length us, event | category | flops | bytes accessed | tf_op | source)
XLA Modules:
  0.0 140.8 jit_solution(2071062645907347346)
XLA Ops:
  0.0 0.1 pad_add_fusion
  0.1 0.8 multiply_add_fusion
  0.9 1.3 select_reduce_fusion.tab
  2.2 136.7 %shard_map.82 = bf16[32,8192]{1,0:T(8,128)(2,1)} custom-call(s32[2,64]{1,0:T(2,128)} %select_reduce_fusion.tab, bf16[256,512]{1,0:T(8,128)(2,1)} %q_ref.1, bf16[256,256]{1,0:T(8,128)(2,1)} %nkv_ref.1, bf16[32,8192]{1,0:T(8,128)(2,1)} %res_ref.1, bf16[24,256,256]{2,1,0:T(8,128)(2,1)} %store_ref.1, bf16[512,8192]{1,0:T(8,128)(2,1)} %w_ref.1), custom_call_target="tpu_custom_call" | custom-call | tf_op jit(solution)/shard_map/pallas_call | solution.py:515
  138.9 1.9 %copy.12 = bf16[32,8192]{1,0:T(8,128)(2,1)} copy(bf16[32,8192]{1,0:T(8,128)(2,1)} %shard_map.82) | data formatting | bytes 1048576
  (1 shorter events, 0.0 us)

commit v5 on v4

--- a/solution.py
+++ b/solution.py
@@ -207,6 +207,7 @@
     res_copy.start()
     w_own.start()
     stage_r(0)
+    stage_r(1)
 
     key = lax.broadcasted_iota(jnp.int32, (BLOCK, NEW), 0)
 
@@ -258,6 +259,10 @@
             p_2(s, 0, j).start()
             p_2(s, 1, j).start()
 
+        @pl.when(jnp.logical_and(s >= 1, s + 1 < SLOTS))
+        def _():
+            stage_r(s + 1)
+
         @pl.when(s == 0)
         def _():
             for z in others:
@@ -269,10 +274,6 @@
         for j in range(2):
             p_1(s, 0, 2 + j).start()
             p_1(s, 1, j).start()
-
-        @pl.when(s + 1 < SLOTS)
-        def _():
-            stage_r(s + 1)
 
         for j in range(2):
             attend(s, up, j)
@@ -468,10 +469,11 @@
 
         stage(stage_c, t)
         stage(stage_h, t - 1)
+        stage(stage_f, jnp.where(t < SLOTS - 1, t - 2, -1))
         stage(stage_m, t)
-        stage(stage_f, t - 2)
-        stage(stage_d, t - 5)
+        stage(stage_f, jnp.where(t < SLOTS - 1, -1, t - 2))
         stage(stage_o, t - 2)
+        stage(stage_d, jnp.where(t < SLOTS, t - 4, jnp.where(t > SLOTS, SLOTS - 4, -1)))
         stage(stage_x, t - 3)
         stage(stage_e, t - 7)
 

time: 141 us -> 135 us (0.957)
  the two profiles are of different devices: /device:TPU:101 before, /device:TPU:4 now
where the time goes in v5:
time: 135 us
  Pallas kernels  131 us (97%)
  other arithmetic  2.2 us (2%)
  local copies, waits for them, and re-layouts  1.87 us (1%)
    pallas_call x1, Pallas kernels, layer(): pl.pallas_call(layer_kernel, out_shape=jax.ShapeDtypeStruct(residual.shap...  131 us

profile of v5, /device:TPU:4, one launch (start us, length us, event | category | flops | bytes accessed | tf_op | source)
XLA Modules:
  0.0 134.9 jit_solution(1314458114187184802)
XLA Ops:
  0.0 0.1 pad_add_fusion
  0.1 0.8 multiply_add_fusion
  0.9 1.3 select_reduce_fusion.tab
  2.2 130.8 %shard_map.82 = bf16[32,8192]{1,0:T(8,128)(2,1)} custom-call(s32[2,64]{1,0:T(2,128)} %select_reduce_fusion.tab, bf16[256,512]{1,0:T(8,128)(2,1)} %q_ref.1, bf16[256,256]{1,0:T(8,128)(2,1)} %nkv_ref.1, bf16[32,8192]{1,0:T(8,128)(2,1)} %res_ref.1, bf16[24,256,256]{2,1,0:T(8,128)(2,1)} %store_ref.1, bf16[512,8192]{1,0:T(8,128)(2,1)} %w_ref.1), custom_call_target="tpu_custom_call" | custom-call | tf_op jit(solution)/shard_map/pallas_call | solution.py:517
  133.0 1.9 %copy.12 = bf16[32,8192]{1,0:T(8,128)(2,1)} copy(bf16[32,8192]{1,0:T(8,128)(2,1)} %shard_map.82) | data formatting | bytes 1048576
  (1 shorter events, 0.0 us)

commit v6 on v5

--- a/solution.py
+++ b/solution.py
@@ -54,11 +54,11 @@
 def layer_kernel(
     tab, q_ref, nkv_ref, res_ref, store_ref, w_ref, out_ref,
     kv_ref, qsrc, qbuf, k_sib, vt_own, vt_sib, nkv, part, r2, r1, rz, att,
-    w, res_sib, proj, x1, x2, zout, zin, done, fin,
+    w, proj, x1, x2, zout, zin, sout, sin,
     kv_send, kv_recv, local,
     qs_send, qz_send, qz_recv, qy_send, qy_recv, qr_send, qr_recv,
     p2_send, p2_recv, p1_send, p1_recv, pz_send, pz_recv, at_send, at_recv,
-    x1_send, x1_recv, x2_send, x2_recv, zh_send, zh_recv, fin_send, fin_recv,
+    x1_send, x1_recv, x2_send, x2_recv, zh_send, zh_recv, si_send, si_recv,
 ):
     kv_own = pltpu.make_async_copy(store_ref, kv_ref, local.at[2])
     kv_own.start()
@@ -93,7 +93,8 @@
     barrier = pltpu.get_barrier_semaphore()
     partners = [{"pool": dev(my, z, c)} for z in others for c in range(2)]
     partners += [{"pool": p} for p in (dev(my, mz, sib), dev(up, mz, core), dev(down, mz, core))]
-    partners += [{"tp": p} for p in (tp_of(pair, zh), tp_of(facing, zh), tp_of(mx, 1 - zh))]
+    partners += [{"tp": p} for p in (tp_of(pair, zh), tp_of(facing, zh))]
+    partners += [{"pool": dev(my, mz, c), "tp": tp_of(mx, 1 - zh)} for c in range(2)]
     for p in partners:
         pl.semaphore_signal(barrier, inc=1, device_id=p, device_id_type=MESH)
 
@@ -146,35 +147,33 @@
     nk_copy = remote(nkv_ref, nkv.at[core], kv_send.at[0], kv_recv.at[0], pool=here)
     k_copy = remote(kv_ref.at[:, :, pl.ds(0, HEAD)], k_sib, kv_send.at[1], kv_recv.at[1], pool=here)
     v_copy = remote(vt_own, vt_sib, kv_send.at[2], kv_recv.at[2], pool=here)
-    res_copy = remote(res_ref.at[:, columns(sib)], res_sib, kv_send.at[3], kv_recv.at[3], pool=here)
     nk_own = pltpu.make_async_copy(nkv_ref, nkv.at[core], local.at[0])
     w_own = pltpu.make_async_copy(w_ref.at[:, columns(core)], w, local.at[1])
 
     def q_y(s, d, z):
         piece = qbuf.at[s, my, z]
-        return remote(piece, piece, qy_send, qy_recv.at[s, d, z], pool=dev((up, down)[d], mz, core))
+        passed = lax.div(z, 2) if d == 0 else 1 - lax.div(z, 2)
+        return remote(piece, piece, qy_send, qy_recv.at[s, d, passed], pool=dev((up, down)[d], mz, core))
 
     def q_relay(s, d, j):
         to, of = ((up, down), (down, up))[d]
         piece = qbuf.at[s, of, 2 * d + j]
-        return remote(piece, piece, qr_send, qr_recv.at[s, d, j], pool=dev(to, mz, core))
+        return remote(piece, piece, qr_send, qr_recv.at[s], pool=dev(to, mz, core))
 
     def z_arrived(s, z):
         wait_into(qbuf.at[s, my, z], qz_recv.at[s, z])
         q_y(s, 0, z).start()
         q_y(s, 1, z).start()
 
-    def y_arrived(s, d, z):
-        wait_into(qbuf.at[s, (down, up)[d], z], qy_recv.at[s, d, z])
-
-    def relay_two(s, j):
+    def y_arrived(s, d, passed):
+        first = 2 * d if passed == 0 else 2 - 2 * d
+        wait_into(qbuf.at[s, (down, up)[d], pl.ds(first, 2)], qy_recv.at[s, d, passed])
+
+    def stage_r(s):
         for d in range(2):
-            y_arrived(s, d, 2 * d + j)
-            q_relay(s, d, j).start()
-
-    def stage_r(s):
-        for j in range(2):
-            relay_two(s, j)
+            y_arrived(s, d, 0)
+            for j in range(2):
+                q_relay(s, d, j).start()
 
     per_core = SLOTS // 2
 
@@ -204,7 +203,6 @@
         z_arrived(0, z)
         z_arrived(1, z)
     send_z(1)
-    res_copy.start()
     w_own.start()
     stage_r(0)
     stage_r(1)
@@ -233,25 +231,28 @@
     def p_2(s, d, j):
         return remote(
             part.at[s, across, 2 * d + j], r2.at[s, d, j],
-            p2_send, p2_recv.at[s, d, j], pool=dev((up, down)[d], mz, core),
+            p2_send, p2_recv.at[s, d], pool=dev((up, down)[d], mz, core),
         )
 
     def p_1(s, d, z):
         to = (up, down)[d]
         return remote(
-            part.at[s, to, z], r1.at[s, d, z], p1_send, p1_recv.at[s, d, z], pool=dev(to, mz, core)
-        )
-
-    def p_z(s, z):
-        return remote(
-            part.at[s, my, z], rz.at[s, mz], pz_send, pz_recv.at[s, mz], pool=dev(my, z, core)
-        )
+            part.at[s, to, z], r1.at[s, d, z], p1_send, p1_recv.at[s, d], pool=dev(to, mz, core)
+        )
+
+    def p_z(s, k):
+        z = others[k]
+        return remote(part.at[s, my, z], rz.at[s, k], pz_send, pz_recv.at[s], pool=dev(my, z, core))
 
     def stage_c(s):
-        for j in range(2):
-            for d in range(2):
-                wait_into(qbuf.at[s, across, 2 * d + j], qr_recv.at[s, d, j])
-                y_arrived(s, d, 2 - 2 * d + j)
+        @pl.when(s == 0)
+        def _():
+            for z in range(NZ):
+                attend(s, my, z)
+
+        for d in range(2):
+            y_arrived(s, d, 1)
+        wait_into(qbuf.at[s, across], qr_recv.at[s])
 
         for z in range(NZ):
             attend(s, across, z)
@@ -278,15 +279,16 @@
         for j in range(2):
             attend(s, up, j)
             attend(s, down, 2 + j)
-        for z in range(NZ):
-            attend(s, my, z)
+        @pl.when(s > 0)
+        def _():
+            for z in range(NZ):
+                attend(s, my, z)
 
     def stage_m(s):
-        @pl.loop(0, 2)
-        def _(j):
-            for d in range(2):
+        for d in range(2):
+            wait_into(r2.at[s, d], p2_recv.at[s, d])
+            for j in range(2):
                 z, to = 2 * d + j, (up, down)[d]
-                wait_into(r2.at[s, d, j], p2_recv.at[s, d, j])
                 put(part, (s, to, z), *merge([get(part, (s, to, z)), get(r2, (s, d, j))]))
                 p_1(s, d, z).start()
 
@@ -304,16 +306,12 @@
             send_z(lax.div(s, 2) + 2)
 
     def stage_h(s):
-        @pl.loop(0, NZ)
-        def _(k):
-            z = lax.rem(mz + 1 + k, NZ)
-            for d in range(2):
-                wait_into(r1.at[s, d, z], p1_recv.at[s, d, z])
+        for d in range(2):
+            wait_into(r1.at[s, d], p1_recv.at[s, d])
+        for k, z in enumerate((*others, mz)):
             put(part, (s, my, z), *merge([get(part, (s, my, z)), get(r1, (s, 0, z)), get(r1, (s, 1, z))]))
-
-            @pl.when(k < NZ - 1)
-            def _():
-                p_z(s, z).start()
+            if k < NZ - 1:
+                p_z(s, k).start()
 
     def fresh(s):
         q = qbuf[s, my, mz]
@@ -333,9 +331,8 @@
 
     def stage_f(s):
         parts = [fresh(s), get(part, (s, my, mz))]
-        for z in others:
-            wait_into(rz.at[s, z], pz_recv.at[s, z])
-            parts.append(get(rz, (s, z)))
+        wait_into(rz.at[s], pz_recv.at[s])
+        parts += [get(rz, (s, k)) for k in range(NZ - 1)]
         o, _, l = merge(parts)
         o = o / l
         o = o.T
@@ -366,13 +363,17 @@
     def x_2(s, n):
         return remote(
             proj.at[s, rows(1 - sent_half(s)), cols(n)], x2.at[s, :, cols(n)],
-            x2_send, x2_recv.at[s, n], tp=tp_of(facing, zh),
+            x2_send, x2_recv.at[lax.div(s, 2), n], tp=tp_of(facing, zh),
         )
 
     def z_h(s, n):
         return remote(
-            zout.at[s, :, cols(n)], zin.at[s, :, cols(n)], zh_send, zh_recv.at[s, n], tp=tp_of(mx, 1 - zh)
-        )
+            zout.at[s, :, cols(n)], zin.at[s, core, :, cols(n)], zh_send, zh_recv.at[share(s), core, n],
+            pool=dev(my, mz, owner(s)), tp=tp_of(mx, 1 - zh),
+        )
+
+    def s_in(s, n):
+        return remote(sout.at[s, :, cols(n)], sin.at[s, :, cols(n)], si_send, si_recv.at[share(s), n], pool=here)
 
     def stage_o(s):
         @pl.when(s == 0)
@@ -409,56 +410,45 @@
         def _():
             keep = 1 - sent_half(s)
 
+            def total(n, z):
+                t = f32(proj[s, part_of(keep, z), cols(n)])
+                return t + f32(x1[s, part_of(0, z), cols(n)]) + f32(x2[s, part_of(0, z), cols(n)])
+
             @pl.loop(0, CHUNKS)
             def _(n):
                 wait_into(x1.at[s, :, cols(n)], x1_recv.at[s, n])
-                wait_into(x2.at[s, :, cols(n)], x2_recv.at[s, n])
-                z = 1 - zh
-                total = f32(proj[s, part_of(keep, z), cols(n)])
-                total += f32(x1[s, part_of(0, z), cols(n)]) + f32(x2[s, part_of(0, z), cols(n)])
-                zout[s, :, cols(n)] = total.astype(jnp.bfloat16)
+                wait_into(x2.at[s, :, cols(n)], x2_recv.at[lax.div(s, 2), n])
+                zout[s, :, cols(n)] = total(n, 1 - zh).astype(jnp.bfloat16)
                 z_h(s, n).start()
 
-    def fin_copy(g):
-        return remote(done.at[g], fin.at[g], fin_send, fin_recv.at[g], pool=here)
+                @pl.when(owner(s) != core)
+                def _():
+                    sout[s, :, cols(n)] = total(n, zh).astype(jnp.bfloat16)
+                    s_in(s, n).start()
 
     def stage_e(s):
-        @pl.when(is_dest(s))
+        @pl.when(jnp.logical_and(is_dest(s), owner(s) == core))
         def _():
             keep = 1 - sent_half(s)
-            mine = owner(s) == core
-            g = share(s)
-            out_rows = pl.ds(pl.multiple_of(g * PART, PART), PART)
-
-            def total(n):
-                wait_into(zin.at[s, :, cols(n)], zh_recv.at[s, n])
-                t = f32(proj[s, part_of(keep, zh), cols(n)]) + f32(zin[s, :, cols(n)])
-                return t + f32(x1[s, part_of(0, zh), cols(n)]) + f32(x2[s, part_of(0, zh), cols(n)])
-
-            def at(n):
-                return pl.ds(pl.multiple_of(core * width + n * chunk, chunk), chunk)
-
-            @pl.when(mine)
-            def _():
-                @pl.loop(0, CHUNKS)
-                def _(n):
-                    out_ref[out_rows, at(n)] = (total(n) + f32(res_ref[out_rows, at(n)])).astype(jnp.bfloat16)
-
-            @pl.when(jnp.logical_not(mine))
-            def _():
-                @pl.loop(0, CHUNKS)
-                def _(n):
-                    done[g, :, cols(n)] = (total(n) + f32(res_sib[out_rows, cols(n)])).astype(jnp.bfloat16)
-
-                fin_copy(g).start()
+            out_rows = pl.ds(pl.multiple_of(share(s) * PART, PART), PART)
+
+            @pl.loop(0, CHUNKS)
+            def _(n):
+                own = f32(proj[s, part_of(keep, zh), cols(n)])
+                own += f32(x1[s, part_of(0, zh), cols(n)]) + f32(x2[s, part_of(0, zh), cols(n)])
+                wait_into(sin.at[s, :, cols(n)], si_recv.at[share(s), n])
+                for c, t in ((core, own), (sib, f32(sin[s, :, cols(n)]))):
+                    wait_into(zin.at[s, c, :, cols(n)], zh_recv.at[share(s), c, n])
+                    at = pl.ds(pl.multiple_of(c * width + n * chunk, chunk), chunk)
+                    t += f32(zin[s, c, :, cols(n)]) + f32(res_ref[out_rows, at])
+                    out_ref[out_rows, at] = t.astype(jnp.bfloat16)
 
     nk_own.wait()
-    for copy in (k_copy, nk_copy, v_copy, res_copy):
+    for copy in (k_copy, nk_copy, v_copy):
         copy.wait_send()
     wait_into(nkv.at[sib], kv_recv.at[0])
     wait_into(k_sib, kv_recv.at[1])
     wait_into(vt_sib, kv_recv.at[2])
-    wait_into(res_sib, kv_recv.at[3])
 
     @pl.loop(0, SLOTS + 2)
     def _(t):
@@ -497,23 +487,18 @@
         (x1, x1_send),
         (x2.at[pl.ds(0, SLOTS // 2)], x2_send),
         (zout.at[pl.ds(0, SLOTS // 2)], zh_send),
-        (fin, fin_send),
+        (sout.at[pl.ds(0, SLOTS // 4)], si_send),
     ):
         wait_into(ref, sem)
-    for g in range(2):
-        wait_into(fin.at[g], fin_recv.at[g])
-        out_ref[g * PART : (g + 1) * PART, columns(sib)] = fin[g]
-
 
 def layer(tab, queries, nkv, store, residual, weight):
     bf = jnp.bfloat16
     blocks = store.shape[0]
     depth, width = weight.shape[0], weight.shape[1] // 2
-    rows = residual.shape[0]
     vmem = pl.BlockSpec(memory_space=pltpu.VMEM)
     dma = pltpu.SemaphoreType.DMA
     unit = (ROWS, NEW)
-    one, each = dma(()), dma((SLOTS, CHUNKS))
+    one = dma(())
     return pl.pallas_call(
         layer_kernel,
         out_shape=jax.ShapeDtypeStruct(residual.shape, bf),
@@ -530,23 +515,23 @@
             pltpu.VMEM((SLOTS, NY, NZ) + unit, bf),
             pltpu.VMEM((SLOTS, 2, 2) + unit, bf),
             pltpu.VMEM((SLOTS, 2, NZ) + unit, bf),
-            pltpu.VMEM((SLOTS, NZ) + unit, bf),
+            pltpu.VMEM((SLOTS, NZ - 1) + unit, bf),
             pltpu.VMEM((SLOTS, 4 * PART, 4 * HEAD), bf),
             pltpu.VMEM((depth, width), bf),
-            pltpu.VMEM((rows, width), bf),
             pltpu.VMEM((SLOTS, 4 * PART, width), bf),
             pltpu.VMEM((SLOTS, 2 * PART, width), bf),
             pltpu.VMEM((SLOTS, 2 * PART, width), bf),
             pltpu.VMEM((SLOTS, PART, width), bf),
+            pltpu.VMEM((SLOTS, 2, PART, width), bf),
             pltpu.VMEM((SLOTS, PART, width), bf),
-            pltpu.VMEM((2, PART, width), bf),
-            pltpu.VMEM((2, PART, width), bf),
-            dma((4,)), dma((4,)), dma((3,)),
+            pltpu.VMEM((SLOTS, PART, width), bf),
+            dma((3,)), dma((3,)), dma((3,)),
             one, one, dma((SLOTS, NZ)),
-            one, dma((SLOTS, 2, NZ)), one, dma((SLOTS, 2, 2)),
-            one, dma((SLOTS, 2, 2)), one, dma((SLOTS, 2, NZ)),
-            one, dma((SLOTS, NZ)), one, dma((SLOTS,)),
-            one, each, one, each, one, each, one, dma((2,)),
+            one, dma((SLOTS, 2, 2)), one, dma((SLOTS,)),
+            one, dma((SLOTS, 2)), one, dma((SLOTS, 2)),
+            one, dma((SLOTS,)), one, dma((SLOTS,)),
+            one, dma((SLOTS, CHUNKS)), one, dma((SLOTS // 2, CHUNKS)),
+            one, dma((2, 2, CHUNKS)), one, dma((2, CHUNKS)),
         ],
         compiler_params=pltpu.CompilerParams(
             collective_id=0, has_side_effects=True, vmem_limit_bytes=56 * 1024 * 1024

time: 135 us -> 132 us (0.978)
  the two profiles are of different devices: /device:TPU:4 before, /device:TPU:36 now
where the time goes in v6:
time: 132 us
  Pallas kernels  128 us (97%)
  other arithmetic  2.2 us (2%)
  local copies, waits for them, and re-layouts  1.87 us (1%)
    pallas_call x1, Pallas kernels, layer(): pl.pallas_call(layer_kernel, out_shape=jax.ShapeDtypeStruct(residual.shap...  128 us

profile of v6, /device:TPU:36, one launch (start us, length us, event | category | flops | bytes accessed | tf_op | source)
XLA Modules:
  0.0 131.8 jit_solution(13325839615071485306)
XLA Ops:
  0.0 0.1 pad_add_fusion
  0.1 0.8 multiply_add_fusion
  0.9 1.3 %select_reduce_fusion.tab = s32[2,64]{1,0:T(2,128)} fusion(s32[64,16]{0,1:T(8,128)S(1)} %multiply_add_fusion, s32[64,16]{0,1:T(8,128)} %param.13, s32[2]{0:T(128)S(1)} %pad_add_fusion), kind=kLoop, calls=%fused_computation | loop fusion | flops 6016 | bytes 8712 | tf_op jit(solution)/shard_map/reduce_sum | solution.py:547
  2.2 127.7 %shard_map.82 = bf16[32,8192]{1,0:T(8,128)(2,1)} custom-call(s32[2,64]{1,0:T(2,128)} %select_reduce_fusion.tab, bf16[256,512]{1,0:T(8,128)(2,1)} %q_ref.1, bf16[256,256]{1,0:T(8,128)(2,1)} %nkv_ref.1, bf16[32,8192]{1,0:T(8,128)(2,1)} %res_ref.1, bf16[24,256,256]{2,1,0:T(8,128)(2,1)} %store_ref.1, bf16[512,8192]{1,0:T(8,128)(2,1)} %w_ref.1), custom_call_target="tpu_custom_call" | custom-call | tf_op jit(solution)/shard_map/pallas_call | solution.py:502
  129.9 1.9 %copy.12 = bf16[32,8192]{1,0:T(8,128)(2,1)} copy(bf16[32,8192]{1,0:T(8,128)(2,1)} %shard_map.82) | data formatting | bytes 1048576
  (1 shorter events, 0.0 us)

commit v7 on v6

--- a/solution.py
+++ b/solution.py
@@ -117,10 +117,10 @@
         return lax.rem(s, 2)
 
     def which(s):
-        return lax.rem(lax.div(s, 2) + lax.rem(s, 2), 2)
+        return lax.rem(lax.rem(s, 2) + lax.div(s, 4), 2)
 
     def share(s):
-        return lax.div(s, 4)
+        return lax.rem(lax.div(s, 2), 2)
 
     def tokens(i):
         return pl.ds(pl.multiple_of(i * NEW, NEW), NEW)
@@ -128,20 +128,20 @@
     def q_z(j, k, c):
         s = 2 * j + core
         return remote(
-            qsrc.at[which(s), lax.div(j, 2), c], qbuf.at[s, my, mz],
+            qsrc.at[which(s), share(s), c], qbuf.at[s, my, mz],
             qz_send, qz_recv.at[s, mz], pool=dev(my, others[k], c),
         )
 
     def q_sib(j):
         s = 2 * j + core
         return remote(
-            qsrc.at[which(s), j // 2, sib], qbuf.at[s, my, mz],
+            qsrc.at[which(s), share(s), sib], qbuf.at[s, my, mz],
             qs_send, qz_recv.at[s, mz], pool=dev(my, mz, sib),
         )
 
     def q_own(j):
         s = 2 * j + core
-        return pltpu.make_async_copy(qsrc.at[which(s), j // 2, core], qbuf.at[s, my, mz], qz_recv.at[s, mz])
+        return pltpu.make_async_copy(qsrc.at[which(s), share(s), core], qbuf.at[s, my, mz], qz_recv.at[s, mz])
 
     here = dev(my, mz, sib)
     nk_copy = remote(nkv_ref, nkv.at[core], kv_send.at[0], kv_recv.at[0], pool=here)
@@ -467,8 +467,9 @@
         stage(stage_x, t - 3)
         stage(stage_e, t - 7)
 
+    stage_d(SLOTS - 3)
     stage_x(SLOTS - 1)
-    for s in range(SLOTS - 3, SLOTS):
+    for s in range(SLOTS - 2, SLOTS):
         stage_d(s)
 
     @pl.loop(SLOTS - 5, SLOTS)

time: 132 us -> 129 us (0.977)
  the two profiles are of different devices: /device:TPU:36 before, /device:TPU:4 now
where the time goes in v7:
time: 129 us
  Pallas kernels  125 us (97%)
  other arithmetic  2.2 us (2%)
  local copies, waits for them, and re-layouts  1.87 us (1%)
    pallas_call x1, Pallas kernels, layer(): pl.pallas_call(layer_kernel, out_shape=jax.ShapeDtypeStruct(residual.shap...  125 us

profile of v7, /device:TPU:4, one launch (start us, length us, event | category | flops | bytes accessed | tf_op | source)
XLA Modules:
  0.0 128.8 jit_solution(1144352417089373331)
XLA Ops:
  0.0 0.1 pad_add_fusion
  0.1 0.8 multiply_add_fusion
  0.9 1.3 %select_reduce_fusion.tab = s32[2,64]{1,0:T(2,128)} fusion(s32[64,16]{0,1:T(8,128)S(1)} %multiply_add_fusion, s32[64,16]{0,1:T(8,128)} %param.13, s32[2]{0:T(128)S(1)} %pad_add_fusion), kind=kLoop, calls=%fused_computation | loop fusion | flops 6016 | bytes 8712 | tf_op jit(solution)/shard_map/reduce_sum | solution.py:548
  2.2 124.7 %shard_map.82 = bf16[32,8192]{1,0:T(8,128)(2,1)} custom-call(s32[2,64]{1,0:T(2,128)} %select_reduce_fusion.tab, bf16[256,512]{1,0:T(8,128)(2,1)} %q_ref.1, bf16[256,256]{1,0:T(8,128)(2,1)} %nkv_ref.1, bf16[32,8192]{1,0:T(8,128)(2,1)} %res_ref.1, bf16[24,256,256]{2,1,0:T(8,128)(2,1)} %store_ref.1, bf16[512,8192]{1,0:T(8,128)(2,1)} %w_ref.1), custom_call_target="tpu_custom_call" | custom-call | tf_op jit(solution)/shard_map/pallas_call | solution.py:503
  126.9 1.9 %copy.12 = bf16[32,8192]{1,0:T(8,128)(2,1)} copy(bf16[32,8192]{1,0:T(8,128)(2,1)} %shard_map.82) | data formatting | bytes 1048576
  (1 shorter events, 0.0 us)

commit v8 on v7

--- a/solution.py
+++ b/solution.py
@@ -187,7 +187,7 @@
         q_sib(j).start()
         if j == 0:
             send_z(0)
-    for s in range(4):
+    for s in range(SLOTS):
         z_arrived(s, mz)
     nk_own.start()
     nk_copy.start()
@@ -291,10 +291,6 @@
                 z, to = 2 * d + j, (up, down)[d]
                 put(part, (s, to, z), *merge([get(part, (s, to, z)), get(r2, (s, d, j))]))
                 p_1(s, d, z).start()
-
-        @pl.when(s + 4 < SLOTS)
-        def _():
-            z_arrived(s + 4, mz)
 
         @pl.when(s + 3 < SLOTS)
         def _():

time: 129 us -> 127 us (0.984)
  Pallas kernels: 125 us -> 122 us
    pallas_call x1, Pallas kernels: 125 us -> 122 us  [layer(): pl.pallas_call(layer_kernel, out_shape=jax.ShapeDtypeStruct(residual.shap...]
where the time goes in v8:
time: 127 us; the launch traced here: 126 us
  Pallas kernels  122 us (96%)
  other arithmetic  2.2 us (2%)
  local copies, waits for them, and re-layouts  1.87 us (1%)
    pallas_call x1, Pallas kernels, layer(): pl.pallas_call(layer_kernel, out_shape=jax.ShapeDtypeStruct(residual.shap...  122 us

profile of v8, /device:TPU:4, one launch (start us, length us, event | category | flops | bytes accessed | tf_op | source)
XLA Modules:
  0.0 125.7 jit_solution(11643576678785648421)
XLA Ops:
  0.0 0.1 pad_add_fusion
  0.1 0.8 multiply_add_fusion
  0.9 1.3 %select_reduce_fusion.tab = s32[2,64]{1,0:T(2,128)} fusion(s32[64,16]{0,1:T(8,128)S(1)} %multiply_add_fusion, s32[64,16]{0,1:T(8,128)} %param.13, s32[2]{0:T(128)S(1)} %pad_add_fusion), kind=kLoop, calls=%fused_computation | loop fusion | flops 6016 | bytes 8712 | tf_op jit(solution)/shard_map/reduce_sum | solution.py:544
  2.2 121.7 %shard_map.82 = bf16[32,8192]{1,0:T(8,128)(2,1)} custom-call(s32[2,64]{1,0:T(2,128)} %select_reduce_fusion.tab, bf16[256,512]{1,0:T(8,128)(2,1)} %q_ref.1, bf16[256,256]{1,0:T(8,128)(2,1)} %nkv_ref.1, bf16[32,8192]{1,0:T(8,128)(2,1)} %res_ref.1, bf16[24,256,256]{2,1,0:T(8,128)(2,1)} %store_ref.1, bf16[512,8192]{1,0:T(8,128)(2,1)} %w_ref.1), custom_call_target="tpu_custom_call" | custom-call | tf_op jit(solution)/shard_map/pallas_call | solution.py:499
  123.9 1.9 %copy.12 = bf16[32,8192]{1,0:T(8,128)(2,1)} copy(bf16[32,8192]{1,0:T(8,128)(2,1)} %shard_map.82) | data formatting | bytes 1048576
  (1 shorter events, 0.0 us)

commit v9 on v8

--- a/solution.py
+++ b/solution.py
@@ -456,9 +456,10 @@
         stage(stage_c, t)
         stage(stage_h, t - 1)
         stage(stage_f, jnp.where(t < SLOTS - 1, t - 2, -1))
+        stage(stage_o, jnp.where(t < SLOTS - 1, t - 2, -1))
         stage(stage_m, t)
         stage(stage_f, jnp.where(t < SLOTS - 1, -1, t - 2))
-        stage(stage_o, t - 2)
+        stage(stage_o, jnp.where(t < SLOTS - 1, -1, t - 2))
         stage(stage_d, jnp.where(t < SLOTS, t - 4, jnp.where(t > SLOTS, SLOTS - 4, -1)))
         stage(stage_x, t - 3)
         stage(stage_e, t - 7)

time: 127 us -> 130 us (1.024)
  Pallas kernels: 122 us -> 125 us
    pallas_call x1, Pallas kernels: 122 us -> 125 us  [layer(): pl.pallas_call(layer_kernel, out_shape=jax.ShapeDtypeStruct(residual.shap...]
where the time goes in v9:
time: 130 us; the launch traced here: 129 us
  Pallas kernels  125 us (96%)
  other arithmetic  2.2 us (2%)
  local copies, waits for them, and re-layouts  1.87 us (1%)
    pallas_call x1, Pallas kernels, layer(): pl.pallas_call(layer_kernel, out_shape=jax.ShapeDtypeStruct(residual.shap...  125 us

profile of v9, /device:TPU:4, one launch (start us, length us, event | category | flops | bytes accessed | tf_op | source)
XLA Modules:
  0.0 129.4 jit_solution(7702446073883697846)
XLA Ops:
  0.0 0.1 pad_add_fusion
  0.1 0.8 multiply_add_fusion
  0.9 1.3 %select_reduce_fusion.tab = s32[2,64]{1,0:T(2,128)} fusion(s32[64,16]{0,1:T(8,128)S(1)} %multiply_add_fusion, s32[64,16]{0,1:T(8,128)} %param.13, s32[2]{0:T(128)S(1)} %pad_add_fusion), kind=kLoop, calls=%fused_computation | loop fusion | flops 6016 | bytes 8712 | tf_op jit(solution)/shard_map/reduce_sum | solution.py:545
  2.2 125.3 %shard_map.82 = bf16[32,8192]{1,0:T(8,128)(2,1)} custom-call(s32[2,64]{1,0:T(2,128)} %select_reduce_fusion.tab, bf16[256,512]{1,0:T(8,128)(2,1)} %q_ref.1, bf16[256,256]{1,0:T(8,128)(2,1)} %nkv_ref.1, bf16[32,8192]{1,0:T(8,128)(2,1)} %res_ref.1, bf16[24,256,256]{2,1,0:T(8,128)(2,1)} %store_ref.1, bf16[512,8192]{1,0:T(8,128)(2,1)} %w_ref.1), custom_call_target="tpu_custom_call" | custom-call | tf_op jit(solution)/shard_map/pallas_call | solution.py:500
  127.5 1.9 %copy.12 = bf16[32,8192]{1,0:T(8,128)(2,1)} copy(bf16[32,8192]{1,0:T(8,128)(2,1)} %shard_map.82) | data formatting | bytes 1048576
  (1 shorter events, 0.0 us)
